TPU v7x, 128 devices: a whole 4x4x4 slice. The times are simulated.
128 devices in a mesh: dp: 4 (over y_lo, core), ctx: 32 (over z, y_hi, x).
Axes of the slice: x: 4, y: 4 (y_hi: 2, y_lo: 2; y = y_hi * 2 + y_lo), z: 4, core: 2. Of those that a mesh axis runs over, the one named last changes fastest.
Arguments:
- normed_layer_input: bfloat16 [4, 6144, 8192], P('dp', 'ctx'), may hold values from -18 to 18
- query: bfloat16 [4, 6144, 8192], P('dp', 'ctx'), may hold values from -9 to 9
- saved_key_value: bfloat16 [4, 6144, 2048], P('dp', 'ctx'), may hold values from -12 to 12
- output_gradient: bfloat16 [4, 6144, 8192], P('dp', 'ctx'), may hold values from -6 to 6
- adapter_down_weight: bfloat16 [24, 8192], replicated, may hold values from -0.0625 to 0.0625
- adapter_up_weight: bfloat16 [8, 10240], replicated, may hold values from -0.09375 to 0.09375
- shifted_head_flags: int32 [8], replicated, may hold values from 0 to 1, as said below
Outputs:
- grad_proj: bfloat16 [4, 6144, 10240], P('dp', 'ctx')
- grad_down: float32 [24, 8192], P(None, 'ctx')
- grad_up: float32 [8, 10240], P(None, 'ctx')
- grad_norm: float32 [], replicated
Inputs may be any that keep to these rules, and one draw needn't show every extreme that they name: `shifted_head_flags`: exactly 4 entries are 1, the others 0.
All inputs are finite; a program needn't handle non-finite values.
Results may differ from a plain program's by a relative error of at most 0.0067.
Values may be sent and summed in bfloat16 or wider, within the bound.
A program may use at most 128 MiB of HBM per device.

v0:
```python
import math

import jax
import jax.numpy as jnp
from jax import lax
from jax.sharding import PartitionSpec as P

HQ = 64
KVH = 8
HD = 128
ADAPTER_RANK = 8
GROUP_DEV = 4


rope_base = 10000.0
adapter_scale = 2.0


def passed_along(block, axis, distance):
    devices = range(lax.axis_size(axis))
    route = [((i - distance) % len(devices), i) for i in devices]
    return lax.ppermute(block, axis, route)


def rotary_tables(positions):
    freqs = jnp.exp(jnp.arange(HD // 2, dtype=jnp.float32) * (-2.0 * math.log(rope_base) / HD))
    angles = positions[:, None] * freqs[None, :]
    return (jnp.cos(angles), jnp.sin(angles))


def rotary_back(grads, cosines, sines):
    first = grads[..., : HD // 2]
    second = grads[..., HD // 2 :]
    cosine = cosines[:, None, :]
    sine = sines[:, None, :]
    return jnp.concatenate(
        [first * cosine + second * sine, second * cosine - first * sine], axis=-1
    )


def local(
    normed_layer_input,
    query,
    saved_key_value,
    output_gradient,
    adapter_down_weight,
    adapter_up_weight,
    shifted_head_flags,
):
    rows = query.shape[1]
    group_heads = HQ // KVH
    width_kv = KVH * HD
    place = lax.axis_index("ctx")
    depth = GROUP_DEV - 1
    span = GROUP_DEV * rows
    scale = HD ** (-0.5)
    own = saved_key_value[0]
    fetched = {}
    for distance in range(1, GROUP_DEV):
        fetched[distance] = passed_along(own, "ctx", distance)
    window = jnp.concatenate([fetched[later] for later in range(depth, 0, -1)] + [own], axis=0)
    keys_all = jnp.moveaxis(window[:, :width_kv].reshape(span, KVH, HD), 1, 0)
    values_all = jnp.moveaxis(window[:, width_kv:].reshape(span, KVH, HD), 1, 0)
    queries = jnp.moveaxis(query[0].reshape(rows, KVH, group_heads, HD), 1, 0)
    grads = jnp.moveaxis(output_gradient[0].reshape(rows, KVH, group_heads, HD), 1, 0)
    key_pos = jnp.arange(span)[None, :]
    query_pos = depth * rows + jnp.arange(rows)[:, None]

    def head_work(packed):
        query_head, key_head, value_head, grad_head, flag = packed
        rank = (place - flag * (GROUP_DEV // 2)) % GROUP_DEV
        lowest = (depth - rank) * rows
        allowed = ((key_pos <= query_pos) & (key_pos >= lowest))[None]
        scores = (
            jnp.einsum("ihd,jd->hij", query_head, key_head, preferred_element_type=jnp.float32)
            * scale
        )
        masked = jnp.where(allowed, scores, -1e30)
        peak = jnp.max(masked, axis=-1, keepdims=True)
        weights = jnp.exp(masked - peak)
        probs = weights / jnp.sum(weights, axis=-1, keepdims=True)
        probs_low = probs.astype(jnp.bfloat16)
        grad_value = jnp.einsum(
            "hij,ihd->jd", probs_low, grad_head, preferred_element_type=jnp.float32
        )
        grad_probs = jnp.einsum(
            "ihd,jd->hij", grad_head, value_head, preferred_element_type=jnp.float32
        )
        inner = jnp.sum(probs * grad_probs, axis=-1, keepdims=True)
        grad_scores = (probs * (grad_probs - inner)).astype(jnp.bfloat16)
        grad_query = (
            jnp.einsum("hij,jd->ihd", grad_scores, key_head, preferred_element_type=jnp.float32)
            * scale
        )
        grad_key = (
            jnp.einsum("hij,ihd->jd", grad_scores, query_head, preferred_element_type=jnp.float32)
            * scale
        )
        return (grad_query, grad_key, grad_value)

    query_terms, key_terms, value_terms = lax.map(
        head_work, (queries, keys_all, values_all, grads, shifted_head_flags)
    )
    partial_value = jnp.concatenate(
        [
            jnp.moveaxis(key_terms, 0, 1).reshape(span, width_kv),
            jnp.moveaxis(value_terms, 0, 1).reshape(span, width_kv),
        ],
        axis=-1,
    )

    def block(distance):
        return partial_value[(depth - distance) * rows : (depth - distance + 1) * rows]

    returned = block(0)
    for distance in range(1, GROUP_DEV):
        returned = returned + passed_along(block(distance), "ctx", -distance)
    positions = (place * rows + jnp.arange(rows)).astype(jnp.float32)
    cosines, sines = rotary_tables(positions)
    grad_query = rotary_back(jnp.moveaxis(query_terms, 0, 1).reshape(rows, HQ, HD), cosines, sines)
    grad_key = rotary_back(returned[:, :width_kv].reshape(rows, KVH, HD), cosines, sines)
    combined = jnp.concatenate(
        [
            grad_query.reshape(rows, HQ * HD),
            grad_key.reshape(rows, width_kv),
            returned[:, width_kv:],
        ],
        axis=-1,
    ).astype(jnp.bfloat16)
    flattened_inputs = normed_layer_input[0]
    down_reduced = lax.dot_general(
        flattened_inputs,
        adapter_down_weight,
        (((1,), (1,)), ((), ())),
        preferred_element_type=jnp.float32,
    ).astype(jnp.bfloat16)
    width_q = HQ * HD
    edges = [(0, width_q), (width_q, width_kv), (width_q + width_kv, width_kv)]
    up_pieces_list, down_pieces_list = ([], [])
    for segment, (column_offset, piece_width) in enumerate(edges):
        gradient_piece = combined[:, column_offset : column_offset + piece_width]
        reduced_piece = down_reduced[:, segment * ADAPTER_RANK : (segment + 1) * ADAPTER_RANK]
        up_pieces_list.append(
            adapter_scale
            * lax.dot_general(
                reduced_piece,
                gradient_piece,
                (((0,), (0,)), ((), ())),
                preferred_element_type=jnp.float32,
            )
        )
        blended_product = lax.dot_general(
            gradient_piece,
            adapter_up_weight[:, column_offset : column_offset + piece_width],
            (((1,), (1,)), ((), ())),
            preferred_element_type=jnp.float32,
        ).astype(jnp.bfloat16)
        down_pieces_list.append(
            adapter_scale
            * lax.dot_general(
                blended_product,
                flattened_inputs,
                (((0,), (0,)), ((), ())),
                preferred_element_type=jnp.float32,
            )
        )
    down_terms = jnp.concatenate(down_pieces_list, axis=0)
    up_terms = jnp.concatenate(up_pieces_list, axis=1)
    total_down, total_up = lax.psum((down_terms, up_terms), ("dp", "ctx"))
    grad_norm = jnp.sqrt(jnp.sum(total_down * total_down) + jnp.sum(total_up * total_up))
    count = lax.axis_size("ctx")
    down_width = total_down.shape[1] // count
    up_width = total_up.shape[1] // count
    share_down = lax.dynamic_slice_in_dim(total_down, place * down_width, down_width, 1)
    share_up = lax.dynamic_slice_in_dim(total_up, place * up_width, up_width, 1)
    return (combined[None], share_down, share_up, grad_norm)


def solution(mesh):
    return jax.shard_map(
        local,
        mesh=mesh,
        in_specs=(
            P("dp", "ctx", None),
            P("dp", "ctx", None),
            P("dp", "ctx", None),
            P("dp", "ctx", None),
            P(),
            P(),
            P(),
        ),
        out_specs=(P("dp", "ctx", None), P(None, "ctx"), P(None, "ctx"), P()),
        check_vma=False,
    )
```

profile of v0, /device:TPU:1, one launch (start us, length us, event | category | flops | bytes accessed | tf_op | source)
XLA Modules:
  0.0 543.8 jit_solution(5727438057804158337)
XLA Ops:
  7.2 3.6 collective-permute-start.1
  10.9 3.5 collective-permute-start
  17.2 4.7 copy.50
  21.9 2.5 copy.51
  27.1 7.5 %collective-permute-done.1 = bf16[192,2048]{1,0:T(8,128)(2,1)} collective-permute-done((bf16[192,2048]{1,0:T(8,128)(2,1)}, bf16[192,2048]{1,0:T(8,128)(2,1)}, u32[]{:S(2)}, u32[]{:S(2)}) %collective-permute-start.1) | collective-permute-done | bytes 786464 | tf_op jit(solution)/shard_map/ppermute | solution.py:22
  36.9 31.0 %collective-permute-done = bf16[192,2048]{1,0:T(8,128)(2,1)} collective-permute-done((bf16[192,2048]{1,0:T(8,128)(2,1)}, bf16[192,2048]{1,0:T(8,128)(2,1)}, u32[]{:S(2)}, u32[]{:S(2)}) %collective-permute-start) | collective-permute-done | bytes 786464 | tf_op jit(solution)/shard_map/ppermute | solution.py:22
  72.4 3.5 pad_maximum_fusion.1
  77.8 163.3 %while.18 = (s32[]{:T(128)}, f32[8,192,8,128]{3,1,2,0:T(8,128)}, f32[8,768,128]{2,1,0:T(8,128)}, f32[8,768,128]{2,1,0:T(8,128)}, bf16[8,768,128]{1,2,0:T(8,128)(...) while((s32[]{:T(128)}, f32[8,192,8,128]{3,1,2,0:T(8,128)}, ...), condition=%wide.region_4.5_spmd.clone.clone, body=%wide.region_0.4_spmd.clone.clone.sunk | while | flops 1525874944 | bytes 61481364 | solution.py:101
  81.8 4.9 fusion.117
  86.8 4.5 fusion.122
  95.6 2.6 fusion.120
  102.2 4.9 fusion.117
  107.2 4.5 fusion.122
  116.0 2.6 fusion.120
  122.7 4.9 fusion.117
  127.6 4.5 fusion.122
  136.5 2.6 fusion.120
  143.1 4.9 fusion.117
  148.0 4.5 fusion.122
  156.9 2.6 fusion.120
  163.5 4.9 fusion.117
  168.4 4.5 fusion.122
  177.3 2.6 fusion.120
  183.9 4.9 fusion.117
  188.9 4.5 fusion.122
  197.7 2.6 fusion.120
  204.3 4.9 fusion.117
  209.3 4.5 fusion.122
  218.1 2.6 fusion.120
  224.8 4.9 fusion.117
  229.7 4.5 fusion.122
  238.6 2.6 fusion.120
  241.2 2.5 bitcast_dynamic-update-slice_fusion.1
  244.4 2.5 fusion.92
  248.4 4.1 collective-permute-start.5
  252.5 11.0 %fusion.91 = (f32[192,64,64]{2,0,1:T(8,128)}, f32[192,64,64]{2,0,1:T(8,128)}) fusion(f32[192,64,128]{2,0,1:T(8,128)} %bitcast.198), kind=kLoop, calls=%fused_computation.108 | loop fusion | bytes 12582912 | tf_op jit(solution)/shard_map/slice | solution.py:32
  263.5 17.3 %multiply_add_fusion = (bf16[192,64,64]{2,1,0:T(8,128)(2,1)S(1)}, bf16[192,64,64]{2,1,0:T(8,128)(2,1)S(1)}) fusion(f32[192,64,64]{2,0,1:T(8,128)} %get-tuple-element.264, f32[192,64,64]{2,0,1:T(8,128)} %get-tuple-element.263, f32[192,64]{1,0:T(8,128)S(1)} %copy-done.9, f32[192,64]{1,0:T(8,128)S(1)} %copy-done.8), kind=kLoop, calls=%fused_computation.57 | loop fusion | flops 6291456 | bytes 9535488 | tf_op jit(solution)/shard_map/add | solution.py:37
  280.9 3.4 maximum_convert_fusion
  284.3 5.8 %concatenate.38 = bf16[1,192,8192]{2,1,0:T(8,128)(2,1)} reshape(bf16[192,64,128]{2,1,0:T(8,128)(2,1)} %maximum_convert_fusion) | data formatting | bytes 6291456 | tf_op jit(solution)/shard_map/concatenate | solution.py:122
  290.1 4.4 convolution_multiply_fusion.1
  294.5 5.8 %convolution_multiply_fusion.4 = f32[8,8192]{1,0:T(8,128)} fusion(bf16[1,192,8192]{2,1,0:T(8,128)(2,1)S(1)} %copy-done, bf16[24,8,64,128]{3,2,1,0:T(8,128)(2,1)} %bitcast.197, bf16[8,10240]{1,0:T(8,128)(2,1)S(1)} %copy-done.11), kind=kOutput, calls=%fused_computation.54 | convolution fusion | flops 50398720 | bytes 6684672 | tf_op jit(solution)/shard_map/dot_general | solution.py:160
  300.3 43.6 %collective-permute-done.3 = f32[192,2048]{1,0:T(8,128)} collective-permute-done((f32[192,2048]{1,0:T(8,128)}, f32[192,2048]{1,0:T(8,128)}, u32[]{:S(2)}, u32[]{:S(2)}) %collective-permute-start.3) | collective-permute-done | bytes 1572896 | tf_op jit(solution)/shard_map/ppermute | solution.py:22
  343.9 11.5 %collective-permute-done.4 = f32[192,2048]{1,0:T(8,128)} collective-permute-done((f32[192,2048]{1,0:T(8,128)}, f32[192,2048]{1,0:T(8,128)}, u32[]{:S(2)}, u32[]{:S(2)}) %collective-permute-start.4) | collective-permute-done | bytes 1572896 | tf_op jit(solution)/shard_map/ppermute | solution.py:22
  355.3 3.4 fusion.61
  360.7 2.7 convolution_multiply_fusion.2
  368.1 2.3 convolution_multiply_fusion.3
  375.3 3.6 pad_maximum_fusion
  378.9 149.3 %all-reduce.3.cloned.1.call-done = (f32[24,8192]{1,0:T(8,128)}, f32[8,10240]{1,0:T(8,128)}) async-done(((f32[24,8192]{1,0:T(8,128)}, f32[8,10240]{1,0:T(8,128)}), (f32[24,8192]{1,0:T(8,128)}, f32[8,10240]{1,0:T(8,128)})) %all-reduce.3.cloned.1.call-update) | async-done | bytes 1114128 | tf_op jit(solution)/shard_map/psum | solution.py:169
  (154 shorter events, 96.2 us)
Async XLA Ops:
  7.2 18.4 %copy-start = (bf16[1,192,8192]{2,1,0:T(8,128)(2,1)S(1)}, bf16[1,192,8192]{2,1,0:T(8,128)(2,1)}, u32[]{:S(2)}) copy-start(bf16[1,192,8192]{2,1,0:T(8,128)(2,1)} %param.9) | copy-start | bytes 9437188
  7.2 521.0 %all-reduce.3.cloned.1.call-start = ((), (), s32[]{:S(2)}) async-start(), calls=%async_computation | async-start | bytes 2228224 | tf_op jit(solution)/shard_map/psum | solution.py:169
  7.2 27.4 %collective-permute-start.1 = (bf16[192,2048]{1,0:T(8,128)(2,1)}, bf16[192,2048]{1,0:T(8,128)(2,1)}, u32[]{:S(2)}, u32[]{:S(2)}) collective-permute-start(bf16[192,2048]{1,0:T(8,128)(2,1)} %bitcast.209), channel_id=1, source_target_pairs={{30,0},{31,1},{0,2},{1,3},{2,4},{3,5},{4,6},{5,7},{6,8},{7,9},{8,1... | collective-permute-start | bytes 2359304 | tf_op jit(solution)/shard_map/ppermute | solution.py:22
  10.9 57.0 %collective-permute-start = (bf16[192,2048]{1,0:T(8,128)(2,1)}, bf16[192,2048]{1,0:T(8,128)(2,1)}, u32[]{:S(2)}, u32[]{:S(2)}) collective-permute-start(bf16[192,2048]{1,0:T(8,128)(2,1)} %bitcast.210), channel_id=1, source_target_pairs={{29,0},{30,1},{31,2},{0,3},{1,4},{2,5},{3,6},{4,7},{5,8},{6,9},{7,... | collective-permute-start | bytes 2359304 | tf_op jit(solution)/shard_map/ppermute | solution.py:22
  14.4 55.8 %collective-permute-start.2 = (bf16[192,2048]{1,0:T(8,128)(2,1)}, bf16[192,2048]{1,0:T(8,128)(2,1)}, u32[]{:S(2)}, u32[]{:S(2)}) collective-permute-start(bf16[192,2048]{1,0:T(8,128)(2,1)} %bitcast.211), channel_id=1, source_target_pairs={{31,0},{0,1},{1,2},{2,3},{3,4},{4,5},{5,6},{6,7},{7,8},{8,9},{9,10... | collective-permute-start | bytes 2359304 | tf_op jit(solution)/shard_map/ppermute | solution.py:22
  17.2 4.7 copy-start.5
  21.9 3.7 copy-start.10
  75.9 1.9 copy-start.13
  86.7 4.5 copy-start.1
  86.8 4.5 copy-start.4
  107.1 4.5 copy-start.1
  107.1 4.5 copy-start.4
  127.6 4.5 copy-start.1
  127.6 4.5 copy-start.4
  148.0 4.5 copy-start.1
  148.0 4.5 copy-start.4
  168.4 4.5 copy-start.1
  168.4 4.5 copy-start.4
  188.9 4.5 copy-start.1
  188.9 4.5 copy-start.4
  209.3 4.5 copy-start.1
  209.3 4.5 copy-start.4
  229.7 4.5 copy-start.1
  229.7 4.5 copy-start.4
  241.2 2.8 copy-start.6
  244.4 4.0 copy-start.2
  248.4 95.4 %collective-permute-start.3 = (f32[192,2048]{1,0:T(8,128)}, f32[192,2048]{1,0:T(8,128)}, u32[]{:S(2)}, u32[]{:S(2)}) collective-permute-start(f32[192,2048]{1,0:T(8,128)} %get-tuple-element.265), channel_id=1, source_target_pairs={{1,0},{2,1},{3,2},{4,3},{5,4},{6,5},{7,6},{8,7},{9,8},{10,9},{11,1... | collective-permute-start | bytes 4718600 | tf_op jit(solution)/shard_map/ppermute | solution.py:22
  248.4 95.4 %collective-permute-start.5 = (f32[192,2048]{1,0:T(8,128)}, f32[192,2048]{1,0:T(8,128)}, u32[]{:S(2)}, u32[]{:S(2)}) collective-permute-start(f32[192,2048]{1,0:T(8,128)} %get-tuple-element.266), channel_id=1, source_target_pairs={{3,0},{4,1},{5,2},{6,3},{7,4},{8,5},{9,6},{10,7},{11,8},{12,9},{13... | collective-permute-start | bytes 4718600 | tf_op jit(solution)/shard_map/ppermute | solution.py:22
  252.5 102.8 %collective-permute-start.4 = (f32[192,2048]{1,0:T(8,128)}, f32[192,2048]{1,0:T(8,128)}, u32[]{:S(2)}, u32[]{:S(2)}) collective-permute-start(f32[192,2048]{1,0:T(8,128)} %get-tuple-element.267), channel_id=1, source_target_pairs={{2,0},{3,1},{4,2},{5,3},{6,4},{7,5},{8,6},{9,7},{10,8},{11,9},{12,... | collective-permute-start | bytes 4718600 | tf_op jit(solution)/shard_map/ppermute | solution.py:22
  252.5 11.0 %copy-start.8 = (f32[192,64]{1,0:T(8,128)S(1)}, f32[192,64]{1,0:T(8,128)}, u32[]{:S(2)}) copy-start(f32[192,64]{1,0:T(8,128)} %get-tuple-element.272) | copy-start | bytes 147460
  252.5 11.0 %copy-start.9 = (f32[192,64]{1,0:T(8,128)S(1)}, f32[192,64]{1,0:T(8,128)}, u32[]{:S(2)}) copy-start(f32[192,64]{1,0:T(8,128)} %get-tuple-element.273) | copy-start | bytes 147460
  284.3 5.8 %copy-start.12 = (bf16[192,24]{0,1:T(8,128)(2,1)S(1)}, bf16[192,24]{0,1:T(8,128)(2,1)}, u32[]{:S(2)}) copy-start(bf16[192,24]{0,1:T(8,128)(2,1)} %fusion.62) | copy-start | bytes 27652
  290.1 4.4 copy-start.11
  358.8 1.1 copy-start.3
  371.4 3.9 copy-start.7
Sparse Core Ops, SparseCore 0:
  375.4 152.7 all-reduce.2
where the time goes:
time: 545 us; the launch traced here: 544 us
  waiting for transfers between devices  243 us (45%)
  matrix products  143 us (26%)
  local copies, waits for them, and re-layouts  70.5 us (13%)
  other arithmetic  54.3 us (10%)
  between operations  16.6 us (3%)
  starting transfers between devices  11.9 us (2%)
    psum x1, waiting for transfers between devices, local(): total_down, total_up = lax.psum((down_terms, up_terms), ('dp', 'ctx'))  149 us
    ppermute x6, waiting for transfers between devices, passed_along(): return lax.ppermute(block, axis, route)  93.5 us
    sub x8, matrix products, head_work(): weights = jnp.exp(masked - peak)  39.5 us
    dot_general x8, matrix products, head_work(): jnp.einsum('hij,ihd->jd', probs_low, grad_head, preferred_element_type=jn...  36 us
    dot_general x8, matrix products, head_work(): jnp.einsum('hij,jd->ihd', grad_scores, key_head, preferred_element_type=j...  20.9 us
    dynamic_slice x16, local copies, waits for them, and re-layouts, local(): lax.map(head_work, (queries, keys_all, values_all, grads, shifted_head_fl...  20.2 us
    add x2, other arithmetic, rotary_back(): first * cosine + second * sine  17.8 us
    unnamed x30, local copies, waits for them, and re-layouts  16.3 us
  transfers between devices with their start and end apart: 7, of which 5 were waited for; matrix products, arithmetic and copies ran while one was open for 13% of the time, Pallas kernels for 0%

commit v1 on v0

v1 whole, which is shorter than its diff:
```python
import functools
import math

import jax
import jax.numpy as jnp
from jax import lax
from jax.experimental import pallas as pl
from jax.experimental.pallas import tpu as pltpu
from jax.sharding import PartitionSpec as P

HQ = 64
KVH = 8
HD = 128
HALF = KVH // 2
GROUP_HEADS = HQ // KVH
ADAPTER_RANK = 8
GROUP_DEV = 4
PACK = 4

rope_base = 10000.0
adapter_scale = 2.0
SCALE = HD ** (-0.5)
SCALE_LOG2 = SCALE * math.log2(math.e)
MESH = pl.DeviceIdType.MESH
VMEM = pl.BlockSpec(memory_space=pltpu.VMEM)
SMEM = pl.BlockSpec(memory_space=pltpu.SMEM)
ANY = pl.BlockSpec(memory_space=pl.ANY)
F32 = jnp.float32
BF16 = jnp.bfloat16


def head_order(flags):
    heads = jnp.arange(KVH)
    shifted = (flags > 0).astype(jnp.int32)
    before = heads[None, :] < heads[:, None]
    ones_before = jnp.sum(jnp.where(before, shifted[None, :], 0), axis=1)
    place = jnp.where(shifted > 0, HALF + ones_before, heads - ones_before)
    return jnp.sum(jnp.where(place[None, :] == heads[:, None], heads[None, :], 0), axis=1)


def dot(a, b, ca, cb):
    return lax.dot_general(a, b, (((ca,), (cb,)), ((), ())), preferred_element_type=F32)


def attention_kernel(
    order,
    q_hbm,
    g_hbm,
    kv_hbm,
    cosines,
    sines,
    dq_hbm,
    dkv,
    kv,
    qv,
    gv,
    window,
    staged,
    returned,
    own,
    dqs,
    kv_sem,
    in_sem,
    out_sem,
    fsend,
    frecv,
    bsend,
    brecv,
):
    rows = q_hbm.shape[0]
    dp = lax.axis_index("dp")
    place = lax.axis_index("ctx")
    count = lax.axis_size("ctx")
    odd = lax.rem(place, 2)
    first = lax.rem(place, GROUP_DEV)
    second = lax.rem(place + 2, GROUP_DEV)
    low_base = jnp.where(first < 2, 0, HALF)
    high_base = HALF - low_base
    width = GROUP_HEADS * HD
    kv_in = [
        pltpu.make_async_copy(kv_hbm.at[:, h * HD : (h + 1) * HD], kv.at[h], kv_sem.at[h])
        for h in range(2 * KVH)
    ]
    copies_in = []
    for h in range(KVH):
        part = slice(h * width, (h + 1) * width)
        copies_in.append(pltpu.make_async_copy(q_hbm.at[:, part], qv.at[h], in_sem.at[0, h]))
        copies_in.append(pltpu.make_async_copy(g_hbm.at[:, part], gv.at[h], in_sem.at[1, h]))
    for copy in kv_in + copies_in:
        copy.start()

    def peer(offset):
        return (dp, lax.rem(place + offset + count, count))

    barrier = pltpu.get_barrier_semaphore()
    for rank in (first, second):
        for step in range(1, GROUP_DEV):
            mate = lax.rem(rank + step, GROUP_DEV)
            pl.semaphore_signal(barrier, inc=1, device_id=peer(mate - rank), device_id_type=MESH)

    for copy in kv_in:
        copy.wait()
    for c in range(KVH):
        rank = first if c < HALF else second
        head = order[c]
        slot = pl.ds(pl.multiple_of(rank * rows, rows), rows)
        window[c, slot, 0:HD] = kv[head]
        window[c, slot, HD : 2 * HD] = kv[head + KVH]

    pl.semaphore_wait(barrier, 2 * (GROUP_DEV - 1))

    def forward(c, rank, distance):
        part = window.at[c, rank * rows : (rank + 1) * rows]
        return pltpu.make_async_remote_copy(
            src_ref=part,
            dst_ref=part,
            send_sem=fsend.at[c, distance - 1],
            recv_sem=frecv.at[c, rank],
            device_id=peer(distance),
            device_id_type=MESH,
        )

    def back(c, rank, target):
        return pltpu.make_async_remote_copy(
            src_ref=staged.at[c, target],
            dst_ref=returned.at[c, rank - 1],
            send_sem=bsend.at[c, target],
            recv_sem=brecv.at[c, rank - 1],
            device_id=peer(target - rank),
            device_id_type=MESH,
        )

    def each_head(step):
        lax.fori_loop(0, HALF, lambda i, _: (step(i), 0)[1], 0)

    def work(c, rank):
        blocks = rank + 1
        span = blocks * rows
        for source in range(rank):
            forward(c, source, rank - source).wait_recv()
        head = order[c]
        keys = window[c, 0:span, 0:HD]
        values = window[c, 0:span, HD : 2 * HD]
        width = PACK * rows
        row = lax.broadcasted_iota(jnp.int32, (rows, width), 0)
        column = lax.rem(lax.broadcasted_iota(jnp.int32, (rows, width), 1), rows)
        allowed = row <= column
        key_sum, value_sum = None, None
        for j in range(GROUP_HEADS // PACK):

            def stacked(ref):
                return jnp.concatenate(
                    [ref[head, :, (j * PACK + t) * HD : (j * PACK + t + 1) * HD] for t in range(PACK)],
                    axis=0,
                )

            queries = stacked(qv)
            grads = stacked(gv)
            scores = dot(keys, queries, 1, 1)
            grad_probs = dot(values, grads, 1, 1)
            last = jnp.where(allowed, scores[span - rows :], -1e30)
            scores = jnp.concatenate([scores[: span - rows], last], axis=0) if rank else last
            peak = jnp.max(scores, axis=0, keepdims=True)
            weights = jnp.exp2((scores - peak) * SCALE_LOG2)
            probs = weights * (1.0 / jnp.sum(weights, axis=0, keepdims=True))
            inner = jnp.sum(probs * grad_probs, axis=0, keepdims=True)
            probs_low = probs.astype(BF16)
            grad_scores = (probs * (grad_probs - inner)).astype(BF16)
            value_term = dot(probs_low, grads, 1, 0)
            key_term = dot(grad_scores, queries, 1, 0)
            value_sum = value_term if value_sum is None else value_sum + value_term
            key_sum = key_term if key_sum is None else key_sum + key_term
            grad_query = dot(grad_scores, keys, 0, 0)
            for t in range(PACK):
                piece = grad_query[t * rows : (t + 1) * rows]
                piece = piece * cosines[...] + pltpu.roll(piece, HD // 2, 1) * sines[...]
                lanes = (j * PACK + t) * HD
                dqs[c, :, lanes : lanes + HD] = piece.astype(BF16)
        pltpu.make_async_copy(dqs.at[c], dq_hbm.at[c], out_sem.at[c]).start()
        for target in range(rank):
            part = slice(target * rows, (target + 1) * rows)
            staged[c, target, :, 0:HD] = key_sum[part].astype(BF16)
            staged[c, target, :, HD : 2 * HD] = value_sum[part].astype(BF16)
            back(c, rank, target).start()
        own[c, :, 0:HD] = key_sum[span - rows :]
        own[c, :, HD : 2 * HD] = value_sum[span - rows :]

    def finish(c, rank):
        total = own[c]
        for sender in range(rank + 1, GROUP_DEV):
            back(c, sender, rank).wait_recv()
            total = total + returned[c, sender - 1].astype(F32)
        keys = total[:, 0:HD]
        keys = keys * cosines[...] + pltpu.roll(keys, HD // 2, 1) * sines[...]
        dkv[c, :, 0:HD] = keys.astype(BF16)
        dkv[c, :, HD : 2 * HD] = total[:, HD : 2 * HD].astype(BF16)

    def phase(low, high):
        sends = [(low_base, low, d) for d in range(1, GROUP_DEV - low)]
        sends += [(high_base, high, d) for d in range(1, GROUP_DEV - high)]
        if low == 0:
            each_head(lambda i: forward(low_base + i, low, 1).start())
            sends = sends[1:]

        def send_all(i):
            for base, rank, distance in sends:
                forward(base + i, rank, distance).start()

        each_head(send_all)
        for copy in copies_in:
            copy.wait()
        each_head(lambda i: work(low_base + i, low))
        each_head(lambda i: work(high_base + i, high))

        def last(i):
            finish(high_base + i, high)
            finish(low_base + i, low)

        each_head(last)

        def drain(i):
            for base, rank in ((low_base, low), (high_base, high)):
                for distance in range(1, GROUP_DEV - rank):
                    forward(base + i, rank, distance).wait_send()
                for target in range(rank):
                    back(base + i, rank, target).wait_send()
                c = base + i
                pltpu.make_async_copy(dqs.at[c], dq_hbm.at[c], out_sem.at[c]).wait()

        each_head(drain)

    pl.when(odd == 0)(lambda: phase(0, 2))
    pl.when(odd == 1)(lambda: phase(1, 3))


def attention(order, query, grads, kv, cosines, sines):
    rows = query.shape[0]
    width = GROUP_HEADS * HD
    return pl.pallas_call(
        attention_kernel,
        out_shape=(
            jax.ShapeDtypeStruct((KVH, rows, width), BF16),
            jax.ShapeDtypeStruct((KVH, rows, 2 * HD), BF16),
        ),
        in_specs=[SMEM, ANY, ANY, ANY, VMEM, VMEM],
        out_specs=(ANY, VMEM),
        scratch_shapes=[
            pltpu.VMEM((2 * KVH, rows, HD), BF16),
            pltpu.VMEM((KVH, rows, width), BF16),
            pltpu.VMEM((KVH, rows, width), BF16),
            pltpu.VMEM((KVH, GROUP_DEV * rows, 2 * HD), BF16),
            pltpu.VMEM((KVH, GROUP_DEV - 1, rows, 2 * HD), BF16),
            pltpu.VMEM((KVH, GROUP_DEV - 1, rows, 2 * HD), BF16),
            pltpu.VMEM((KVH, rows, 2 * HD), F32),
            pltpu.VMEM((KVH, rows, width), BF16),
            pltpu.SemaphoreType.DMA((2 * KVH,)),
            pltpu.SemaphoreType.DMA((2, KVH)),
            pltpu.SemaphoreType.DMA((KVH,)),
            pltpu.SemaphoreType.DMA((KVH, GROUP_DEV - 1)),
            pltpu.SemaphoreType.DMA((KVH, GROUP_DEV - 1)),
            pltpu.SemaphoreType.DMA((KVH, GROUP_DEV - 1)),
            pltpu.SemaphoreType.DMA((KVH, GROUP_DEV - 1)),
        ],
        compiler_params=pltpu.CompilerParams(
            collective_id=0, has_side_effects=True, vmem_limit_bytes=52 * 2**20
        ),
        name="attention_backward",
    )(order, query, grads, kv, cosines, sines)


SHARDS = 32
PIECE = 48
RING = 4


def packed_place(shard):
    z, rest = divmod(shard, 8)
    high, x = divmod(rest, 4)
    return (z * 4 + x) * 2 + high


def adapter_kernel(
    order, x_hbm, dq_hbm, dkv, down_w, up_w, out_hbm, packed, xv, dqv, kvn, up, x_sem, dq_sem, out_sem
):
    width = GROUP_HEADS * HD
    width_q = HQ * HD
    width_kv = KVH * HD
    rank = ADAPTER_RANK
    x_copy = pltpu.make_async_copy(x_hbm, xv, x_sem)
    x_copy.start()

    def dq_copy(c):
        return pltpu.make_async_copy(dq_hbm.at[c], dqv.at[c], dq_sem.at[c])

    def out_copy(c):
        columns = pl.ds(pl.multiple_of(order[c] * width, width), width)
        return pltpu.make_async_copy(dqv.at[c], out_hbm.at[:, columns], out_sem.at[c])

    for c in range(KVH):
        dq_copy(c).start()
    for c in range(KVH):
        head = order[c]
        kvn[:, pl.ds(pl.multiple_of(head * HD, HD), HD)] = dkv[c, :, 0:HD]
        kvn[:, pl.ds(pl.multiple_of((head + KVH) * HD, HD), HD)] = dkv[c, :, HD : 2 * HD]
    kv_copy = pltpu.make_async_copy(
        kvn, out_hbm.at[:, width_q : width_q + 2 * width_kv], out_sem.at[KVH]
    )
    kv_copy.start()
    x_copy.wait()
    low = jnp.transpose(dot(xv[...], down_w[...], 1, 1)).astype(BF16)
    low_q, low_k, low_v = (low[s * rank : (s + 1) * rank] for s in range(3))
    mixed_q = None
    for c in range(KVH):
        dq_copy(c).wait()
        out_copy(c).start()
        columns = pl.ds(pl.multiple_of(order[c] * width, width), width)
        up[:, columns] = adapter_scale * dot(low_q, dqv[c], 1, 0)
        term = dot(dqv[c], up_w[:, columns], 1, 1)
        mixed_q = term if mixed_q is None else mixed_q + term
    up[:, width_q : width_q + width_kv] = adapter_scale * dot(low_k, kvn[:, 0:width_kv], 1, 0)
    up[:, width_q + width_kv :] = adapter_scale * dot(low_v, kvn[:, width_kv:], 1, 0)
    mixed_k = dot(kvn[:, 0:width_kv], up_w[:, width_q : width_q + width_kv], 1, 1)
    mixed_v = dot(kvn[:, width_kv:], up_w[:, width_q + width_kv :], 1, 1)
    mixed = jnp.transpose(jnp.concatenate([mixed_q, mixed_k, mixed_v], axis=1)).astype(BF16)
    down_width = xv.shape[1] // SHARDS
    up_width = up.shape[1] // SHARDS
    zeros = jnp.zeros((8, HD), F32)
    for shard in range(SHARDS):
        down = adapter_scale * dot(mixed, xv[:, shard * down_width : (shard + 1) * down_width], 1, 0)
        mine = up[:, shard * up_width : (shard + 1) * up_width]
        rest = jnp.concatenate(
            [mine[:, 2 * HD :], jnp.zeros((8, 3 * HD - up_width), F32)], axis=1
        )
        at = packed_place(shard)
        packed[0, at] = jnp.concatenate([down[:, 0:HD], mine[:, 0:HD], rest, zeros], 0).astype(BF16)
        packed[1, at] = jnp.concatenate(
            [down[:, HD:], mine[:, HD : 2 * HD], zeros, zeros], 0
        ).astype(BF16)
    for c in range(KVH):
        out_copy(c).wait()
    kv_copy.wait()


def adapters(order, x, dq, dkv, down_w, up_w):
    rows, model = x.shape
    columns = up_w.shape[1]
    return pl.pallas_call(
        adapter_kernel,
        out_shape=(
            jax.ShapeDtypeStruct((rows, columns), BF16),
            jax.ShapeDtypeStruct((2, SHARDS, PIECE, HD), BF16),
        ),
        in_specs=[SMEM, ANY, ANY, VMEM, VMEM, VMEM],
        out_specs=(ANY, VMEM),
        scratch_shapes=[
            pltpu.VMEM((rows, model), BF16),
            pltpu.VMEM(dq.shape, BF16),
            pltpu.VMEM((rows, 2 * KVH * HD), BF16),
            pltpu.VMEM((ADAPTER_RANK, columns), F32),
            pltpu.SemaphoreType.DMA,
            pltpu.SemaphoreType.DMA((KVH,)),
            pltpu.SemaphoreType.DMA((KVH + 1,)),
        ],
        compiler_params=pltpu.CompilerParams(vmem_limit_bytes=48 * 2**20),
        name="adapter_terms",
    )(order, x, dq, dkv, down_w, up_w)


def reduce_kernel(
    packed,
    down_out,
    up_out,
    norm_out,
    got1,
    sum1,
    got2,
    sum2,
    got3,
    halves,
    norms,
    quarters,
    send1,
    recv1,
    send2,
    recv2,
    send3,
    recv3,
    send4,
    recv4,
    send5,
    recv5,
    send6,
    recv6,
):
    dp = lax.axis_index("dp")
    place = lax.axis_index("ctx")
    core = lax.rem(dp, 2)
    y_low = lax.div(dp, 2)
    z = lax.div(place, 8)
    y_high = lax.rem(lax.div(place, 4), 2)
    x = lax.rem(place, 4)
    y = y_high * 2 + y_low
    plane = z * 4 + x

    def device(plane, y, core):
        high, low = lax.div(y, 2), lax.rem(y, 2)
        return (low * 2 + core, lax.div(plane, 4) * 8 + high * 4 + lax.rem(plane, 4))

    def remote(src, dst, send, recv, target):
        return pltpu.make_async_remote_copy(
            src_ref=src,
            dst_ref=dst,
            send_sem=send,
            recv_sem=recv,
            device_id=target,
            device_id_type=MESH,
        )

    def in_plane(step):
        return lax.rem(plane + step, 16)

    def in_ring(step):
        return lax.rem(y + step, RING)

    def quarter_device(step):
        code = lax.rem(core * 2 + y_high + step, 4)
        return device(plane, lax.rem(code, 2) * 2 + y_low, lax.div(code, 2))

    mate = device(plane, y, 1 - core)
    barrier = pltpu.get_barrier_semaphore()

    def greet(target):
        pl.semaphore_signal(barrier, inc=1, device_id=target, device_id_type=MESH)

    greet(mate)
    lax.fori_loop(1, 16, lambda k, _: (greet(device(in_plane(k), y, core)), 0)[1], 0)
    for step in range(1, RING):
        greet(device(plane, in_ring(step), core))
        greet(quarter_device(step))
    pl.semaphore_wait(barrier, 1 + 15 + 2 * (RING - 1))

    first = remote(packed.at[1 - core], got1, send1, recv1, mate)
    first.start()
    first.wait_recv()

    def both(t):
        part = pl.ds(2 * t, 2)
        return packed[core, part].astype(F32) + got1[part].astype(F32)

    def second(k):
        t = in_plane(k)
        part = pl.ds(2 * t, 2)
        return remote(
            sum1.at[part], got2.at[plane], send2.at[k], recv2.at[plane], device(t, y, core)
        )

    def send_second(k, _):
        t = in_plane(k)
        sum1[pl.ds(2 * t, 2)] = both(t).astype(BF16)
        second(k).start()
        return 0

    lax.fori_loop(1, 16, send_second, 0)
    total = both(plane)

    def add_second(k, total):
        source = in_plane(16 - k)
        remote(
            sum1.at[pl.ds(0, 2)], got2.at[source], send2.at[k], recv2.at[source], mate
        ).wait_recv()
        return total + got2[source].astype(F32)

    sum2[...] = lax.fori_loop(1, 16, add_second, total)

    def third(step):
        target = in_ring(step)
        return remote(
            sum2.at[lax.div(target, 2)],
            got3.at[y],
            send3.at[step],
            recv3.at[y],
            device(plane, target, core),
        )

    for step in range(1, RING):
        third(step).start()
    got3[y] = sum2[y_high]
    for step in range(1, RING):
        source = in_ring(step)
        remote(sum2.at[0], got3.at[source], send3.at[step], recv3.at[source], mate).wait_recv()
    mine = got3[0] + got3[1] + got3[2] + got3[3]
    halves[core] = mine
    fourth = remote(halves.at[core], halves.at[core], send4, recv4, mate)
    fourth.start()
    squares = mine * mine
    norms[plane] = functools.reduce(
        lambda a, b: a + b, [squares[8 * r : 8 * (r + 1)] for r in range(PIECE // 8)]
    )

    def fifth(k):
        return remote(
            norms.at[plane], norms.at[plane], send5.at[k], recv5.at[plane], device(in_plane(k), y, core)
        )

    def fifth_arrival(k):
        source = in_plane(k)
        return remote(norms.at[source], norms.at[source], send5.at[k], recv5.at[source], mate)

    lax.fori_loop(1, 16, lambda k, _: (fifth(k).start(), 0)[1], 0)
    lax.fori_loop(1, 16, lambda k, _: (fifth_arrival(k).wait_recv(), 0)[1], 0)
    code = core * 2 + y_high
    quarters[code] = jnp.sum(norms[...], axis=0)

    def sixth(step):
        return remote(
            quarters.at[code], quarters.at[code], send6.at[step], recv6.at[code], quarter_device(step)
        )

    for step in range(1, 4):
        sixth(step).start()
    remote(halves.at[core], halves.at[1 - core], send4, recv4, mate).wait_recv()
    down_out[:, 0:HD] = halves[0, 0:24]
    down_out[:, HD : 2 * HD] = halves[1, 0:24]
    up_out[:, 0:HD] = halves[0, 24:32]
    up_out[:, HD : 2 * HD] = halves[1, 24:32]
    up_out[:, 2 * HD :] = halves[0, 32:40, 0 : up_out.shape[1] - 2 * HD]
    for step in range(1, 4):
        source = lax.rem(code + step, 4)
        remote(
            quarters.at[source], quarters.at[source], send6.at[step], recv6.at[source], mate
        ).wait_recv()
    everything = jnp.sum(jnp.sum(quarters[...], axis=0), keepdims=True)
    norm_out[...] = jnp.broadcast_to(jnp.sqrt(everything), norm_out.shape)

    first.wait_send()
    fourth.wait_send()
    lax.fori_loop(1, 16, lambda k, _: (second(k).wait_send(), 0)[1], 0)
    lax.fori_loop(1, 16, lambda k, _: (fifth(k).wait_send(), 0)[1], 0)
    for step in range(1, 4):
        third(step).wait_send()
        sixth(step).wait_send()


def reduced(packed):
    dma = pltpu.SemaphoreType.DMA
    return pl.pallas_call(
        reduce_kernel,
        out_shape=(
            jax.ShapeDtypeStruct((24, 256), F32),
            jax.ShapeDtypeStruct((8, 320), F32),
            jax.ShapeDtypeStruct((8, HD), F32),
        ),
        in_specs=[VMEM],
        out_specs=(VMEM, VMEM, VMEM),
        scratch_shapes=[
            pltpu.VMEM((SHARDS, PIECE, HD), BF16),
            pltpu.VMEM((SHARDS, PIECE, HD), BF16),
            pltpu.VMEM((16, 2, PIECE, HD), BF16),
            pltpu.VMEM((2, PIECE, HD), F32),
            pltpu.VMEM((RING, PIECE, HD), F32),
            pltpu.VMEM((2, PIECE, HD), F32),
            pltpu.VMEM((16, 8, HD), F32),
            pltpu.VMEM((4, 8, HD), F32),
            dma,
            dma,
            dma((16,)),
            dma((16,)),
            dma((RING,)),
            dma((RING,)),
            dma,
            dma,
            dma((16,)),
            dma((16,)),
            dma((4,)),
            dma((4,)),
        ],
        compiler_params=pltpu.CompilerParams(
            collective_id=1, has_side_effects=True, vmem_limit_bytes=32 * 2**20
        ),
        name="adapter_sums",
    )(packed)


def rotary_tables(positions):
    freqs = jnp.exp(jnp.arange(HD // 2, dtype=F32) * (-2.0 * math.log(rope_base) / HD))
    angles = positions[:, None] * freqs[None, :]
    return (jnp.cos(angles), jnp.sin(angles))


def local(
    normed_layer_input,
    query,
    saved_key_value,
    output_gradient,
    adapter_down_weight,
    adapter_up_weight,
    shifted_head_flags,
):
    rows = query.shape[1]
    place = lax.axis_index("ctx")
    positions = (place * rows + jnp.arange(rows)).astype(F32)
    cosines, sines = rotary_tables(positions)
    cosines = jnp.concatenate([cosines, cosines], axis=1) * SCALE
    sines = jnp.concatenate([sines, -sines], axis=1) * SCALE
    order = head_order(shifted_head_flags)
    dq, dkv = attention(
        order, query[0], output_gradient[0], saved_key_value[0], cosines, sines
    )
    grad_proj, packed = adapters(
        order, normed_layer_input[0], dq, dkv, adapter_down_weight, adapter_up_weight
    )
    grad_down, grad_up, norm = reduced(packed)
    return (grad_proj[None], grad_down, grad_up, norm[0, 0])


def solution(mesh):
    return jax.shard_map(
        local,
        mesh=mesh,
        in_specs=(
            P("dp", "ctx", None),
            P("dp", "ctx", None),
            P("dp", "ctx", None),
            P("dp", "ctx", None),
            P(),
            P(),
            P(),
        ),
        out_specs=(P("dp", "ctx", None), P(None, "ctx"), P(None, "ctx"), P()),
        check_vma=False,
    )
```

time: 545 us -> 91.4 us (0.17)
  waiting for transfers between devices: 243 us -> 0 us
  matrix products: 143 us -> 0 us
  Pallas kernels: 0 us -> 85.5 us
  local copies, waits for them, and re-layouts: 70.5 us -> 2.86 us
  other arithmetic: 54.3 us -> 2.11 us
  between operations: 16.6 us -> 0.71 us
  starting transfers between devices: 11.9 us -> 0 us
    psum x1 -> x0, waiting for transfers between devices: 149 us -> none  [local(): total_down, total_up = lax.psum((down_terms, up_terms), ('dp', 'ctx'))]
    dot_general x39 -> x0, matrix products: 103 us -> none  [the longest x8 36 us: head_work(): jnp.einsum('hij,ihd->jd', probs_low, grad_head, preferred_element_type=jn...]
    ppermute x6 -> x0, waiting for transfers between devices: 93.5 us -> none  [passed_along(): return lax.ppermute(block, axis, route)]
    pallas_call x0 -> x3, Pallas kernels: none -> 85.5 us  [the longest x1 49.6 us: attention(): pl.pallas_call(attention_kernel, out_shape=(jax.ShapeDtypeStruct((KVH, ro...]
    sub x8 -> x0, matrix products: 39.5 us -> none  [head_work(): weights = jnp.exp(masked - peak)]
    dynamic_slice x18 -> x0, local copies, waits for them, and re-layouts: 23 us -> none  [the longest x16 20.2 us: local(): lax.map(head_work, (queries, keys_all, values_all, grads, shifted_head_fl...]
    add x11 -> x0, other arithmetic: 21.2 us -> none  [the longest x2 17.8 us: rotary_back(): first * cosine + second * sine]
    slice x3 -> x1, local copies, waits for them, and re-layouts: 15.3 us -> 0.51 us  [local(): return (grad_proj[None], grad_down, grad_up, norm[0, 0])]
  transfers between devices with their start and end apart: 7 -> 0, of which waited for: 5 -> 0; matrix products, arithmetic and copies ran while one was open for 13% -> 0% of each run, Pallas kernels for 0% -> 0%
where the time goes in v1:
time: 91.4 us; the launch traced here: 91.2 us
  Pallas kernels  85.5 us (94%)
  local copies, waits for them, and re-layouts  2.86 us (3%)
  other arithmetic  2.11 us (2%)
    pallas_call x1, Pallas kernels, attention(): pl.pallas_call(attention_kernel, out_shape=(jax.ShapeDtypeStruct((KVH, ro...  49.6 us
    pallas_call x1, Pallas kernels, reduced(): pl.pallas_call(reduce_kernel, out_shape=(jax.ShapeDtypeStruct((24, 256),...  29.2 us
    pallas_call x1, Pallas kernels, adapters(): pl.pallas_call(adapter_kernel, out_shape=(jax.ShapeDtypeStruct((rows, col...  6.67 us
    unnamed x10, local copies, waits for them, and re-layouts  2.35 us

profile of v1, /device:TPU:1, one launch (start us, length us, event | category | flops | bytes accessed | tf_op | source)
XLA Modules:
  0.0 91.2 jit_solution(3586524097168193982)
XLA Ops:
  0.6 0.7 compare_convert_fusion
  1.3 0.1 select_reduce_fusion.1
  1.4 0.7 compare_select_fusion
  2.1 0.1 select_reduce_fusion.order
  2.2 0.4 multiply_sine_fusion
  2.6 0.1 maximum_multiply_fusion
  2.8 0.0 copy-start.1
  2.8 1.1 %copy-done.1 = bf16[1,192,2048]{2,1,0:T(8,128)(2,1)S(1)} copy-done((bf16[1,192,2048]{2,1,0:T(8,128)(2,1)S(1)}, bf16[1,192,2048]{2,1,0:T(8,128)(2,1)}, u32[]{:S(2)}) %copy-start.1) | copy-done | bytes 786456
  3.9 0.0 copy-start
  3.9 0.0 copy-start.2
  3.9 0.0 copy-start.3
  3.9 49.6 %attention_backward.1 = (bf16[8,192,1024]{2,1,0:T(8,128)(2,1)}, bf16[8,192,256]{2,1,0:T(8,128)(2,1)S(1)}) custom-call(s32[8]{0:T(128)S(1)} %select_reduce_fusion.order, bf16[192,8192]{1,0:T(8,128)(2,1)} %bitcast.8, bf16[192,8192]{1,0:T(8,128)(2,1)} %bitcast.9, bf16[192,2048]{1,0:T(8,128)(2,1)S(1)} %bitcast.7, f32[192,128]{1,0:T(8,128)S(1)} %get-tuple-element.21.cosines, ...), custom_call_target="tpu_custom_call" | custom-call | tf_op jit(solution)/shard_map/attention_backward/pallas_call | solution.py:239
  53.5 0.0 copy-done
  53.6 0.0 copy-done.2
  53.6 0.0 copy-done.3
  53.6 6.7 %adapter_terms.1 = (bf16[192,10240]{1,0:T(8,128)(2,1)}, bf16[2,32,48,128]{3,2,1,0:T(8,128)(2,1)S(1)}) custom-call(s32[8]{0:T(128)S(1)} %select_reduce_fusion.order, bf16[192,8192]{1,0:T(8,128)(2,1)S(1)} %bitcast.6, bf16[8,192,1024]{2,1,0:T(8,128)(2,1)} %get-tuple-element.11.dq_hbm, bf16[8,192,256]{2,1,0:T(8,128)(2,1)S(1)} %get-tuple-element.12.dkv, ...), custom_call_target="tpu_custom_call" | custom-call | tf_op jit(solution)/shard_map/adapter_terms/pallas_call | solution.py:347
  60.3 29.2 %adapter_sums.1 = (f32[24,256]{1,0:T(8,128)S(1)}, f32[8,320]{1,0:T(8,128)S(1)}, f32[8,128]{1,0:T(8,128)S(1)}) custom-call(bf16[2,32,48,128]{3,2,1,0:T(8,128)(2,1)S(1)} %get-tuple-element.14.packed), custom_call_target="tpu_custom_call" | custom-call | tf_op jit(solution)/shard_map/adapter_sums/pallas_call | solution.py:546
  89.5 0.5 slice.3
  90.0 0.6 copy.13
  90.6 0.6 copy.14
  (2 shorter events, 0.0 us)
Async XLA Ops:
  2.8 1.1 %copy-start.1 = (bf16[1,192,2048]{2,1,0:T(8,128)(2,1)S(1)}, bf16[1,192,2048]{2,1,0:T(8,128)(2,1)}, u32[]{:S(2)}) copy-start(bf16[1,192,2048]{2,1,0:T(8,128)(2,1)} %param.9) | copy-start | bytes 2359300
  3.9 49.6 %copy-start = (bf16[1,192,8192]{2,1,0:T(8,128)(2,1)S(1)}, bf16[1,192,8192]{2,1,0:T(8,128)(2,1)}, u32[]{:S(2)}) copy-start(bf16[1,192,8192]{2,1,0:T(8,128)(2,1)} %param.7) | copy-start | bytes 9437188
  3.9 49.6 %copy-start.2 = (bf16[24,8192]{1,0:T(8,128)(2,1)S(1)}, bf16[24,8192]{1,0:T(8,128)(2,1)}, u32[]{:S(2)}) copy-start(bf16[24,8192]{1,0:T(8,128)(2,1)} %down_w.1) | copy-start | bytes 1179652
  3.9 49.7 %copy-start.3 = (bf16[8,10240]{1,0:T(8,128)(2,1)S(1)}, bf16[8,10240]{1,0:T(8,128)(2,1)}, u32[]{:S(2)}) copy-start(bf16[8,10240]{1,0:T(8,128)(2,1)} %up_w.1) | copy-start | bytes 491524

commit v2 on v1

v2 whole, which is shorter than its diff:
```python
import functools
import math

import jax
import jax.numpy as jnp
import numpy as np
from jax import lax
from jax.experimental import pallas as pl
from jax.experimental.pallas import tpu as pltpu
from jax.sharding import PartitionSpec as P

HQ = 64
KVH = 8
HD = 128
HALF = KVH // 2
GROUP_HEADS = HQ // KVH
ADAPTER_RANK = 8
GROUP_DEV = 4
PACK = 4
SHARDS = 32
PIECE = 48
RING = 4
PLANE = 16

rope_base = 10000.0
adapter_scale = 2.0
SCALE = HD ** (-0.5)
SCALE_LOG2 = SCALE * math.log2(math.e)
MESH = pl.DeviceIdType.MESH
VMEM = pl.BlockSpec(memory_space=pltpu.VMEM)
SMEM = pl.BlockSpec(memory_space=pltpu.SMEM)
HBM = pl.BlockSpec(memory_space=pltpu.HBM)
F32 = jnp.float32
BF16 = jnp.bfloat16


def head_at(flags, position):
    ones = jnp.int32(0)
    head = jnp.int32(0)
    for h in range(KVH):
        flag = jnp.minimum(flags[h], 1)
        here = (1 - flag) * (h - ones) + flag * (HALF + ones)
        head = head + h * (here == position).astype(jnp.int32)
        ones = ones + flag
    return head


def positions_of(flags):
    ones = jnp.int32(0)
    found = []
    for h in range(KVH):
        flag = jnp.minimum(flags[h], 1)
        found.append((1 - flag) * (h - ones) + flag * (HALF + ones))
        ones = ones + flag
    return found


def dot(a, b, ca, cb):
    return lax.dot_general(a, b, (((ca,), (cb,)), ((), ())), preferred_element_type=F32)


def packed_place(shard):
    z, rest = divmod(shard, 8)
    high, x = divmod(rest, 4)
    return (z * 4 + x) * 2 + high


def kernel(
    flags,
    x_hbm,
    q_hbm,
    kv_hbm,
    g_hbm,
    down_w,
    up_w,
    row_table,
    block_table,
    grad_proj,
    down_out,
    up_out,
    norm_out,
    xv,
    kv,
    qv,
    gv,
    window,
    staged,
    returned,
    own,
    dqs,
    dkv,
    kvn,
    cosines,
    sines,
    low_t,
    up_heads,
    up,
    up_class,
    mixed_q,
    packed,
    got1,
    sum1,
    got2,
    sum2,
    got3,
    halves,
    norms,
    quarters,
    x_sem,
    kv_sem,
    in_sem,
    fsend,
    frecv,
    bsend,
    brecv,
    send1,
    recv1,
    send2,
    recv2,
    send3,
    recv3,
    send4,
    recv4,
    send5,
    recv5,
    send6,
    recv6,
):
    rows = q_hbm.shape[0]
    dp = lax.axis_index("dp")
    place = lax.axis_index("ctx")
    count = lax.axis_size("ctx")
    odd = lax.rem(place, 2)
    first_rank = lax.rem(place, GROUP_DEV)
    second_rank = lax.rem(place + 2, GROUP_DEV)
    low_base = jnp.where(first_rank < 2, 0, HALF)
    high_base = HALF - low_base
    core = lax.rem(dp, 2)
    y_low = lax.div(dp, 2)
    y_high = lax.rem(lax.div(place, 4), 2)
    y = y_high * 2 + y_low
    plane = lax.div(place, 8) * 4 + lax.rem(place, 4)
    width = GROUP_HEADS * HD
    width_q = HQ * HD
    width_kv = KVH * HD
    rank_a = ADAPTER_RANK

    kv_in = [
        pltpu.make_async_copy(kv_hbm.at[:, h * HD : (h + 1) * HD], kv.at[h], kv_sem.at[h])
        for h in range(2 * KVH)
    ]
    copies_in = []
    for h in range(KVH):
        part = slice(h * width, (h + 1) * width)
        copies_in.append(pltpu.make_async_copy(q_hbm.at[:, part], qv.at[h], in_sem.at[0, h]))
        copies_in.append(pltpu.make_async_copy(g_hbm.at[:, part], gv.at[h], in_sem.at[1, h]))
    x_in = pltpu.make_async_copy(x_hbm, xv, x_sem)
    for copy in kv_in + copies_in:
        copy.start()
    x_in.start()

    def peer(offset):
        return (dp, lax.rem(place + offset + count, count))

    def device(plane, y, core):
        high, low = lax.div(y, 2), lax.rem(y, 2)
        return (low * 2 + core, lax.div(plane, 4) * 8 + high * 4 + lax.rem(plane, 4))

    def in_plane(step):
        return lax.rem(plane + step, PLANE)

    def in_ring(step):
        return lax.rem(y + step, RING)

    def quarter_device(step):
        code = lax.rem(core * 2 + y_high + step, 4)
        return device(plane, lax.rem(code, 2) * 2 + y_low, lax.div(code, 2))

    mate = device(plane, y, 1 - core)
    barrier = pltpu.get_barrier_semaphore()

    def greet(target):
        pl.semaphore_signal(barrier, inc=1, device_id=target, device_id_type=MESH)

    for rank in (first_rank, second_rank):
        for step in range(1, GROUP_DEV):
            greet(peer(lax.rem(rank + step, GROUP_DEV) - rank))
    lax.fori_loop(1, PLANE, lambda k, _: (greet(device(in_plane(k), y, core)), 0)[1], 0)
    for step in range(1, RING):
        greet(device(plane, in_ring(step), core))
        greet(quarter_device(step))
    greet(mate)

    for copy in kv_in:
        copy.wait()
    for c in range(KVH):
        rank = first_rank if c < HALF else second_rank
        head = head_at(flags, c)
        slot = pl.ds(pl.multiple_of(rank * rows, rows), rows)
        window[c, slot, 0:HD] = kv[head]
        window[c, slot, HD : 2 * HD] = kv[head + KVH]

    pl.semaphore_wait(barrier, 2 * (GROUP_DEV - 1) + PLANE - 1 + 2 * (RING - 1) + 1)

    def forward(c, rank, distance):
        part = window.at[c, rank * rows : (rank + 1) * rows]
        return pltpu.make_async_remote_copy(
            src_ref=part,
            dst_ref=part,
            send_sem=fsend.at[c, distance - 1],
            recv_sem=frecv.at[c, rank],
            device_id=peer(distance),
            device_id_type=MESH,
        )

    def back(c, rank, target):
        return pltpu.make_async_remote_copy(
            src_ref=staged.at[c, target],
            dst_ref=returned.at[c, rank - 1],
            send_sem=bsend.at[c, target],
            recv_sem=brecv.at[c, rank - 1],
            device_id=peer(target - rank),
            device_id_type=MESH,
        )

    def each_head(step, start=0, stop=HALF):
        lax.fori_loop(start, stop, lambda i, _: (step(i), 0)[1], 0)

    def sends(low, high):
        if low == 0:
            each_head(lambda i: forward(low_base + i, 0, 1).start(), 0, 2)

        def send_all(i):
            for base, rank in ((low_base, low), (high_base, high)):
                for distance in range(2 if rank == 0 else 1, GROUP_DEV - rank):
                    forward(base + i, rank, distance).start()

        each_head(send_all)
        if low == 0:
            each_head(lambda i: forward(low_base + i, 0, 1).start(), 2, HALF)

    pl.when(odd == 0)(lambda: sends(0, 2))
    pl.when(odd == 1)(lambda: sends(1, 3))

    block_cos, block_sin = block_table[0, pl.ds(place, 1)], block_table[1, pl.ds(place, 1)]
    row_cos, row_sin = row_table[0], row_table[1]
    cosines[...] = block_cos * row_cos - block_sin * row_sin
    sines[...] = block_sin * row_cos + block_cos * row_sin
    for h in range(KVH):
        up_heads[h] = up_w[:, h * width : (h + 1) * width].astype(F32)
    mixed_q[...] = jnp.zeros_like(mixed_q)
    for copy in copies_in:
        copy.wait()
    x_in.wait()
    low_t[...] = jnp.transpose(dot(xv[...], down_w[...], 1, 1))

    def low_of(segment):
        return low_t[segment * rank_a : (segment + 1) * rank_a].astype(BF16)

    def work(c, rank):
        blocks = rank + 1
        span = blocks * rows
        for source in range(rank):
            forward(c, source, rank - source).wait_recv()
        head = head_at(flags, c)
        keys = window[c, 0:span, 0:HD]
        values = window[c, 0:span, HD : 2 * HD]
        packed_rows = PACK * rows
        row = lax.broadcasted_iota(jnp.int32, (rows, packed_rows), 0)
        column = lax.rem(lax.broadcasted_iota(jnp.int32, (rows, packed_rows), 1), rows)
        allowed = row <= column
        key_sum, value_sum = None, None
        for j in range(GROUP_HEADS // PACK):

            def stacked(ref):
                return jnp.concatenate(
                    [ref[head, :, (j * PACK + t) * HD : (j * PACK + t + 1) * HD] for t in range(PACK)],
                    axis=0,
                )

            queries = stacked(qv)
            grads = stacked(gv)
            scores = dot(keys, queries, 1, 1)
            grad_probs = dot(values, grads, 1, 1)
            last = jnp.where(allowed, scores[span - rows :], -1e30)
            scores = jnp.concatenate([scores[: span - rows], last], axis=0) if rank else last
            peak = jnp.max(scores, axis=0, keepdims=True)
            weights = jnp.exp2((scores - peak) * SCALE_LOG2)
            probs = weights * (1.0 / jnp.sum(weights, axis=0, keepdims=True))
            inner = jnp.sum(probs * grad_probs, axis=0, keepdims=True)
            probs_low = probs.astype(BF16)
            grad_scores = (probs * (grad_probs - inner)).astype(BF16)
            value_term = dot(probs_low, grads, 1, 0)
            key_term = dot(grad_scores, queries, 1, 0)
            value_sum = value_term if value_sum is None else value_sum + value_term
            key_sum = key_term if key_sum is None else key_sum + key_term
            grad_query = dot(grad_scores, keys, 0, 0)
            for t in range(PACK):
                piece = grad_query[t * rows : (t + 1) * rows]
                piece = piece * cosines[...] + pltpu.roll(piece, HD // 2, 1) * sines[...]
                lanes = (j * PACK + t) * HD
                dqs[c, :, lanes : lanes + HD] = piece.astype(BF16)
        for target in range(rank):
            part = slice(target * rows, (target + 1) * rows)
            staged[c, target, :, 0:HD] = key_sum[part].astype(BF16)
            staged[c, target, :, HD : 2 * HD] = value_sum[part].astype(BF16)
            back(c, rank, target).start()
        own[c, :, 0:HD] = key_sum[span - rows :]
        own[c, :, HD : 2 * HD] = value_sum[span - rows :]
        up_class[c] = adapter_scale * dot(low_of(0), dqs[c], 1, 0)
        mixed_q[...] += dot(dqs[c], up_heads[head].astype(BF16), 1, 1)

    def finish(c, rank):
        total = own[c]
        for sender in range(rank + 1, GROUP_DEV):
            back(c, sender, rank).wait_recv()
            total = total + returned[c, sender - 1].astype(F32)
        keys = total[:, 0:HD]
        keys = keys * cosines[...] + pltpu.roll(keys, HD // 2, 1) * sines[...]
        dkv[c, :, 0:HD] = keys.astype(BF16)
        dkv[c, :, HD : 2 * HD] = total[:, HD : 2 * HD].astype(BF16)

    def phase(low, high):
        early = HALF if low == 0 else 2

        def step(t):
            is_high = jnp.logical_and(t >= early, t < early + HALF)
            pl.when(is_high)(lambda: work(high_base + t - early, high))
            pl.when(jnp.logical_not(is_high))(
                lambda: work(low_base + jnp.where(t < early, t, t - HALF), low)
            )

        each_head(step, 0, KVH)

    pl.when(odd == 0)(lambda: phase(0, 2))
    pl.when(odd == 1)(lambda: phase(1, 3))

    position = positions_of(flags)
    for h in range(KVH):
        grad_proj[:, h * width : (h + 1) * width] = dqs[position[h]]
        up[:, h * width : (h + 1) * width] = up_class[position[h]]

    def collect(low, high):
        def last(i):
            finish(high_base + i, high)
            finish(low_base + i, low)

        each_head(last)

    pl.when(odd == 0)(lambda: collect(0, 2))
    pl.when(odd == 1)(lambda: collect(1, 3))

    for h in range(KVH):
        kvn[:, h * HD : (h + 1) * HD] = dkv[position[h], :, 0:HD]
        kvn[:, width_kv + h * HD : width_kv + (h + 1) * HD] = dkv[position[h], :, HD : 2 * HD]
    grad_proj[:, width_q : width_q + 2 * width_kv] = kvn[...]
    up[:, width_q : width_q + width_kv] = adapter_scale * dot(low_of(1), kvn[:, 0:width_kv], 1, 0)
    up[:, width_q + width_kv :] = adapter_scale * dot(low_of(2), kvn[:, width_kv:], 1, 0)
    mixed_k = dot(kvn[:, 0:width_kv], up_w[:, width_q : width_q + width_kv], 1, 1)
    mixed_v = dot(kvn[:, width_kv:], up_w[:, width_q + width_kv :], 1, 1)
    mixed = jnp.transpose(jnp.concatenate([mixed_q[...], mixed_k, mixed_v], axis=1)).astype(BF16)
    down_width = xv.shape[1] // SHARDS
    up_width = up.shape[1] // SHARDS
    zeros = jnp.zeros((8, HD), F32)
    for shard in range(SHARDS):
        down = adapter_scale * dot(mixed, xv[:, shard * down_width : (shard + 1) * down_width], 1, 0)
        mine = up[:, shard * up_width : (shard + 1) * up_width]
        rest = jnp.concatenate(
            [mine[:, 2 * HD :], jnp.zeros((8, 3 * HD - up_width), F32)], axis=1
        )
        at = packed_place(shard)
        packed[0, at] = jnp.concatenate([down[:, 0:HD], mine[:, 0:HD], rest, zeros], 0).astype(BF16)
        packed[1, at] = jnp.concatenate(
            [down[:, HD:], mine[:, HD : 2 * HD], zeros, zeros], 0
        ).astype(BF16)

    def remote(src, dst, send, recv, target):
        return pltpu.make_async_remote_copy(
            src_ref=src,
            dst_ref=dst,
            send_sem=send,
            recv_sem=recv,
            device_id=target,
            device_id_type=MESH,
        )

    first = remote(packed.at[1 - core], got1, send1, recv1, mate)
    first.start()
    first.wait_recv()

    def both(t):
        part = pl.ds(2 * t, 2)
        return packed[core, part].astype(F32) + got1[part].astype(F32)

    def second(k):
        t = in_plane(k)
        part = pl.ds(2 * t, 2)
        return remote(
            sum1.at[part], got2.at[plane], send2.at[k], recv2.at[plane], device(t, y, core)
        )

    def send_second(k, _):
        t = in_plane(k)
        sum1[pl.ds(2 * t, 2)] = both(t).astype(BF16)
        second(k).start()
        return 0

    lax.fori_loop(1, PLANE, send_second, 0)
    total = both(plane)

    def add_second(k, total):
        source = in_plane(PLANE - k)
        remote(
            sum1.at[pl.ds(0, 2)], got2.at[source], send2.at[k], recv2.at[source], mate
        ).wait_recv()
        return total + got2[source].astype(F32)

    sum2[...] = lax.fori_loop(1, PLANE, add_second, total)

    def third(step):
        target = in_ring(step)
        return remote(
            sum2.at[lax.div(target, 2)],
            got3.at[y],
            send3.at[step],
            recv3.at[y],
            device(plane, target, core),
        )

    for step in range(1, RING):
        third(step).start()
    got3[y] = sum2[y_high]
    for step in range(1, RING):
        source = in_ring(step)
        remote(sum2.at[0], got3.at[source], send3.at[step], recv3.at[source], mate).wait_recv()
    mine = got3[0] + got3[1] + got3[2] + got3[3]
    halves[core] = mine
    fourth = remote(halves.at[core], halves.at[core], send4, recv4, mate)
    fourth.start()
    squares = mine * mine
    norms[plane] = functools.reduce(
        lambda a, b: a + b, [squares[8 * r : 8 * (r + 1)] for r in range(PIECE // 8)]
    )

    def fifth(k):
        return remote(
            norms.at[plane], norms.at[plane], send5.at[k], recv5.at[plane], device(in_plane(k), y, core)
        )

    def fifth_arrival(k):
        source = in_plane(k)
        return remote(norms.at[source], norms.at[source], send5.at[k], recv5.at[source], mate)

    lax.fori_loop(1, PLANE, lambda k, _: (fifth(k).start(), 0)[1], 0)
    lax.fori_loop(1, PLANE, lambda k, _: (fifth_arrival(k).wait_recv(), 0)[1], 0)
    code = core * 2 + y_high
    quarters[code] = jnp.sum(norms[...], axis=0)

    def sixth(step):
        return remote(
            quarters.at[code], quarters.at[code], send6.at[step], recv6.at[code], quarter_device(step)
        )

    for step in range(1, 4):
        sixth(step).start()
    remote(halves.at[core], halves.at[1 - core], send4, recv4, mate).wait_recv()
    down_out[:, 0:HD] = halves[0, 0:24]
    down_out[:, HD : 2 * HD] = halves[1, 0:24]
    up_out[:, 0:HD] = halves[0, 24:32]
    up_out[:, HD : 2 * HD] = halves[1, 24:32]
    up_out[:, 2 * HD :] = halves[0, 32:40, 0 : up_out.shape[1] - 2 * HD]
    for step in range(1, 4):
        source = lax.rem(code + step, 4)
        remote(
            quarters.at[source], quarters.at[source], send6.at[step], recv6.at[source], mate
        ).wait_recv()
    everything = jnp.sum(jnp.sum(quarters[...], axis=0), keepdims=True)
    norm_out[...] = jnp.broadcast_to(jnp.sqrt(everything), norm_out.shape)

    first.wait_send()
    fourth.wait_send()
    lax.fori_loop(1, PLANE, lambda k, _: (second(k).wait_send(), 0)[1], 0)
    lax.fori_loop(1, PLANE, lambda k, _: (fifth(k).wait_send(), 0)[1], 0)
    for step in range(1, 4):
        third(step).wait_send()
        sixth(step).wait_send()

    def drain(low, high):
        def wait(i):
            for base, rank in ((low_base, low), (high_base, high)):
                for distance in range(1, GROUP_DEV - rank):
                    forward(base + i, rank, distance).wait_send()
                for target in range(rank):
                    back(base + i, rank, target).wait_send()

        each_head(wait)

    pl.when(odd == 0)(lambda: drain(0, 2))
    pl.when(odd == 1)(lambda: drain(1, 3))


def rotary_constants(rows, blocks):
    freqs = rope_base ** (-2.0 * np.arange(HD // 2) / HD)

    def table(positions, scale):
        angles = positions[:, None] * freqs[None, :]
        cosines, sines = np.cos(angles), np.sin(angles)
        both = np.stack(
            [np.concatenate([cosines, cosines], 1), np.concatenate([sines, -sines], 1)]
        )
        return jnp.asarray((both * scale).astype(np.float32))

    return table(np.arange(rows), 1.0), table(np.arange(blocks) * rows, SCALE)


def local(
    normed_layer_input,
    query,
    saved_key_value,
    output_gradient,
    adapter_down_weight,
    adapter_up_weight,
    shifted_head_flags,
):
    rows, model = normed_layer_input.shape[1:]
    columns = adapter_up_weight.shape[1]
    width = GROUP_HEADS * HD
    row_table, block_table = rotary_constants(rows, lax.axis_size("ctx"))
    dma = pltpu.SemaphoreType.DMA
    grad_proj, grad_down, grad_up, norm = pl.pallas_call(
        kernel,
        out_shape=(
            jax.ShapeDtypeStruct((rows, columns), BF16),
            jax.ShapeDtypeStruct((3 * ADAPTER_RANK, model // SHARDS), F32),
            jax.ShapeDtypeStruct((ADAPTER_RANK, columns // SHARDS), F32),
            jax.ShapeDtypeStruct((8, HD), F32),
        ),
        in_specs=[SMEM, HBM, HBM, HBM, HBM, VMEM, VMEM, VMEM, VMEM],
        out_specs=(VMEM, VMEM, VMEM, VMEM),
        scratch_shapes=[
            pltpu.VMEM((rows, model), BF16),
            pltpu.VMEM((2 * KVH, rows, HD), BF16),
            pltpu.VMEM((KVH, rows, width), BF16),
            pltpu.VMEM((KVH, rows, width), BF16),
            pltpu.VMEM((KVH, GROUP_DEV * rows, 2 * HD), BF16),
            pltpu.VMEM((KVH, GROUP_DEV - 1, rows, 2 * HD), BF16),
            pltpu.VMEM((KVH, GROUP_DEV - 1, rows, 2 * HD), BF16),
            pltpu.VMEM((KVH, rows, 2 * HD), F32),
            pltpu.VMEM((KVH, rows, width), BF16),
            pltpu.VMEM((KVH, rows, 2 * HD), BF16),
            pltpu.VMEM((rows, 2 * KVH * HD), BF16),
            pltpu.VMEM((rows, HD), F32),
            pltpu.VMEM((rows, HD), F32),
            pltpu.VMEM((3 * ADAPTER_RANK, rows), F32),
            pltpu.VMEM((KVH, ADAPTER_RANK, width), F32),
            pltpu.VMEM((ADAPTER_RANK, columns), F32),
            pltpu.VMEM((KVH, ADAPTER_RANK, width), F32),
            pltpu.VMEM((rows, ADAPTER_RANK), F32),
            pltpu.VMEM((2, SHARDS, PIECE, HD), BF16),
            pltpu.VMEM((SHARDS, PIECE, HD), BF16),
            pltpu.VMEM((SHARDS, PIECE, HD), BF16),
            pltpu.VMEM((PLANE, 2, PIECE, HD), BF16),
            pltpu.VMEM((2, PIECE, HD), F32),
            pltpu.VMEM((RING, PIECE, HD), F32),
            pltpu.VMEM((2, PIECE, HD), F32),
            pltpu.VMEM((PLANE, 8, HD), F32),
            pltpu.VMEM((4, 8, HD), F32),
            dma,
            dma((2 * KVH,)),
            dma((2, KVH)),
            dma((KVH, GROUP_DEV - 1)),
            dma((KVH, GROUP_DEV - 1)),
            dma((KVH, GROUP_DEV - 1)),
            dma((KVH, GROUP_DEV - 1)),
            dma,
            dma,
            dma((PLANE,)),
            dma((PLANE,)),
            dma((RING,)),
            dma((RING,)),
            dma,
            dma,
            dma((PLANE,)),
            dma((PLANE,)),
            dma((4,)),
            dma((4,)),
        ],
        compiler_params=pltpu.CompilerParams(
            collective_id=0, has_side_effects=True, vmem_limit_bytes=36 * 2**20
        ),
        name="attention_and_adapter_gradients",
    )(
        shifted_head_flags,
        normed_layer_input[0],
        query[0],
        saved_key_value[0],
        output_gradient[0],
        adapter_down_weight,
        adapter_up_weight,
        row_table,
        block_table,
    )
    return (grad_proj[None], grad_down, grad_up, norm[0, 0])


def solution(mesh):
    return jax.shard_map(
        local,
        mesh=mesh,
        in_specs=(
            P("dp", "ctx", None),
            P("dp", "ctx", None),
            P("dp", "ctx", None),
            P("dp", "ctx", None),
            P(),
            P(),
            P(),
        ),
        out_specs=(P("dp", "ctx", None), P(None, "ctx"), P(None, "ctx"), P()),
        check_vma=False,
    )
```

time: 91.4 us -> 92.8 us (1.015)
  local copies, waits for them, and re-layouts: 2.86 us -> 14.7 us
  Pallas kernels: 85.5 us -> 77.1 us
  other arithmetic: 2.11 us -> 0 us
    unnamed x10 -> x21, local copies, waits for them, and re-layouts: 2.35 us -> 14.2 us
    pallas_call x3 -> x1, Pallas kernels: 85.5 us -> 77.1 us  [local(): pl.pallas_call(kernel, out_shape=(jax.ShapeDtypeStruct((rows, columns), B...]
where the time goes in v2:
time: 92.8 us; the launch traced here: 92.4 us
  Pallas kernels  77.1 us (83%)
  local copies, waits for them, and re-layouts  14.7 us (16%)
    pallas_call x1, Pallas kernels, local(): pl.pallas_call(kernel, out_shape=(jax.ShapeDtypeStruct((rows, columns), B...  77.1 us
    unnamed x21, local copies, waits for them, and re-layouts  14.2 us

profile of v2, /device:TPU:1, one launch (start us, length us, event | category | flops | bytes accessed | tf_op | source)
XLA Modules:
  0.0 92.4 jit_solution(16234280655188784010)
XLA Ops:
  0.6 0.0 copy-start
  0.6 1.9 %copy-done = bf16[1,192,8192]{2,1,0:T(8,128)(2,1)S(1)} copy-done((bf16[1,192,8192]{2,1,0:T(8,128)(2,1)S(1)}, bf16[1,192,8192]{2,1,0:T(8,128)(2,1)}, u32[]{:S(2)}) %copy-start) | copy-done | bytes 3145752
  2.5 0.0 copy-start.1
  2.5 1.9 %copy-done.1 = bf16[1,192,8192]{2,1,0:T(8,128)(2,1)S(1)} copy-done((bf16[1,192,8192]{2,1,0:T(8,128)(2,1)S(1)}, bf16[1,192,8192]{2,1,0:T(8,128)(2,1)}, u32[]{:S(2)}) %copy-start.1) | copy-done | bytes 3145752
  4.4 0.0 copy-start.2
  4.4 1.9 %copy-done.2 = bf16[1,192,8192]{2,1,0:T(8,128)(2,1)S(1)} copy-done((bf16[1,192,8192]{2,1,0:T(8,128)(2,1)S(1)}, bf16[1,192,8192]{2,1,0:T(8,128)(2,1)}, u32[]{:S(2)}) %copy-start.2) | copy-done | bytes 3145752
  6.3 0.0 copy-start.3
  6.3 1.1 %copy-done.3 = bf16[1,192,2048]{2,1,0:T(8,128)(2,1)S(1)} copy-done((bf16[1,192,2048]{2,1,0:T(8,128)(2,1)S(1)}, bf16[1,192,2048]{2,1,0:T(8,128)(2,1)}, u32[]{:S(2)}) %copy-start.3) | copy-done | bytes 786456
  7.4 0.0 copy-start.4
  7.4 1.0 %copy-done.4 = bf16[24,8192]{1,0:T(8,128)(2,1)S(1)} copy-done((bf16[24,8192]{1,0:T(8,128)(2,1)S(1)}, bf16[24,8192]{1,0:T(8,128)(2,1)}, u32[]{:S(2)}) %copy-start.4) | copy-done | bytes 393240
  8.4 0.0 copy-start.5
  8.4 0.9 %copy-done.5 = f32[2,192,128]{2,1,0:T(8,128)S(1)} copy-done((f32[2,192,128]{2,1,0:T(8,128)S(1)}, f32[2,192,128]{2,1,0:T(8,128)}, u32[]{:S(2)}) %copy-start.5) | copy-done | bytes 196632
  9.4 0.0 copy-start.6
  9.4 0.9 copy-done.6
  10.3 0.0 copy-start.7
  10.3 0.8 copy-done.7
  11.0 0.0 copy-start.8
  11.0 0.7 copy-done.8
  11.7 77.1 %attention_and_adapter_gradients.1 = (bf16[192,10240]{1,0:T(8,128)(2,1)S(1)}, f32[24,256]{1,0:T(8,128)S(1)}, f32[8,320]{1,0:T(8,128)S(1)}, f32[8,128]{1,0:T(8,128)S(1)}) custom-call(s32[8]{0:T(128)S(1)} %copy-done.8, bf16[192,8192]{1,0:T(8,128)(2,1)S(1)} %bitcast.7, bf16[192,8192]{1,0:T(8,128)(2,1)S(1)} %bitcast.8, bf16[192,2048]{1,0:T(8,128)(2,1)S(1)} %bitcast.10, ...), custom_call_target="tpu_custom_call" | custom-call | tf_op jit(solution)/shard_map/attention_and_adapter_gradients/pallas_call | solution.py:530
  88.8 0.5 slice.3
  89.3 1.9 %copy.16 = bf16[1,192,10240]{2,1,0:T(8,128)(2,1)} copy(bf16[1,192,10240]{2,1,0:T(8,128)(2,1)S(1)} %bitcast.6) | data formatting | bytes 7864320
  91.2 0.6 copy.17
  91.8 0.6 copy.18
Async XLA Ops:
  0.6 1.9 %copy-start = (bf16[1,192,8192]{2,1,0:T(8,128)(2,1)S(1)}, bf16[1,192,8192]{2,1,0:T(8,128)(2,1)}, u32[]{:S(2)}) copy-start(bf16[1,192,8192]{2,1,0:T(8,128)(2,1)} %param.9) | copy-start | bytes 9437188
  2.5 1.9 %copy-start.1 = (bf16[1,192,8192]{2,1,0:T(8,128)(2,1)S(1)}, bf16[1,192,8192]{2,1,0:T(8,128)(2,1)}, u32[]{:S(2)}) copy-start(bf16[1,192,8192]{2,1,0:T(8,128)(2,1)} %param.10) | copy-start | bytes 9437188
  4.4 1.9 %copy-start.2 = (bf16[1,192,8192]{2,1,0:T(8,128)(2,1)S(1)}, bf16[1,192,8192]{2,1,0:T(8,128)(2,1)}, u32[]{:S(2)}) copy-start(bf16[1,192,8192]{2,1,0:T(8,128)(2,1)} %param.12) | copy-start | bytes 9437188
  6.3 1.1 %copy-start.3 = (bf16[1,192,2048]{2,1,0:T(8,128)(2,1)S(1)}, bf16[1,192,2048]{2,1,0:T(8,128)(2,1)}, u32[]{:S(2)}) copy-start(bf16[1,192,2048]{2,1,0:T(8,128)(2,1)} %param.11) | copy-start | bytes 2359300
  7.4 1.0 %copy-start.4 = (bf16[24,8192]{1,0:T(8,128)(2,1)S(1)}, bf16[24,8192]{1,0:T(8,128)(2,1)}, u32[]{:S(2)}) copy-start(bf16[24,8192]{1,0:T(8,128)(2,1)} %down_w.1) | copy-start | bytes 1179652
  8.4 0.9 %copy-start.5 = (f32[2,192,128]{2,1,0:T(8,128)S(1)}, f32[2,192,128]{2,1,0:T(8,128)}, u32[]{:S(2)}) copy-start(f32[2,192,128]{2,1,0:T(8,128)} %constant.4.clone.row_table) | copy-start | bytes 589828
  9.4 0.9 copy-start.6
  10.3 0.8 copy-start.7
  11.0 0.7 copy-start.8

commit v3 on v2

--- a/solution.py
+++ b/solution.py
@@ -71,16 +71,21 @@
     q_hbm,
     kv_hbm,
     g_hbm,
-    down_w,
-    up_w,
-    row_table,
-    block_table,
+    down_hbm,
+    up_hbm,
+    row_hbm,
+    block_hbm,
     grad_proj,
     down_out,
     up_out,
     norm_out,
     xv,
+    kv_rows,
     kv,
+    down_w,
+    up_w,
+    row_table,
+    block_table,
     qv,
     gv,
     window,
@@ -106,6 +111,7 @@
     halves,
     norms,
     quarters,
+    small_sem,
     x_sem,
     kv_sem,
     in_sem,
@@ -145,19 +151,8 @@
     width_kv = KVH * HD
     rank_a = ADAPTER_RANK
 
-    kv_in = [
-        pltpu.make_async_copy(kv_hbm.at[:, h * HD : (h + 1) * HD], kv.at[h], kv_sem.at[h])
-        for h in range(2 * KVH)
-    ]
-    copies_in = []
-    for h in range(KVH):
-        part = slice(h * width, (h + 1) * width)
-        copies_in.append(pltpu.make_async_copy(q_hbm.at[:, part], qv.at[h], in_sem.at[0, h]))
-        copies_in.append(pltpu.make_async_copy(g_hbm.at[:, part], gv.at[h], in_sem.at[1, h]))
-    x_in = pltpu.make_async_copy(x_hbm, xv, x_sem)
-    for copy in kv_in + copies_in:
-        copy.start()
-    x_in.start()
+    kv_in = pltpu.make_async_copy(kv_hbm, kv_rows, kv_sem)
+    kv_in.start()
 
     def peer(offset):
         return (dp, lax.rem(place + offset + count, count))
@@ -191,8 +186,23 @@
         greet(quarter_device(step))
     greet(mate)
 
-    for copy in kv_in:
-        copy.wait()
+    copies_in = []
+    for h in range(KVH):
+        part = slice(h * width, (h + 1) * width)
+        copies_in.append(pltpu.make_async_copy(q_hbm.at[:, part], qv.at[h], in_sem.at[0, h]))
+        copies_in.append(pltpu.make_async_copy(g_hbm.at[:, part], gv.at[h], in_sem.at[1, h]))
+    small_in = [
+        pltpu.make_async_copy(source, target, small_sem.at[i])
+        for i, (source, target) in enumerate(
+            [(row_hbm, row_table), (block_hbm, block_table), (up_hbm, up_w), (down_hbm, down_w)]
+        )
+    ]
+    x_in = pltpu.make_async_copy(x_hbm, xv, x_sem)
+    kv_in.wait()
+    for copy in copies_in + small_in + [x_in]:
+        copy.start()
+    for h in range(2 * KVH):
+        kv[h] = kv_rows[:, h * HD : (h + 1) * HD]
     for c in range(KVH):
         rank = first_rank if c < HALF else second_rank
         head = head_at(flags, c)
@@ -242,6 +252,8 @@
     pl.when(odd == 0)(lambda: sends(0, 2))
     pl.when(odd == 1)(lambda: sends(1, 3))
 
+    for copy in small_in:
+        copy.wait()
     block_cos, block_sin = block_table[0, pl.ds(place, 1)], block_table[1, pl.ds(place, 1)]
     row_cos, row_sin = row_table[0], row_table[1]
     cosines[...] = block_cos * row_cos - block_sin * row_sin
@@ -530,16 +542,21 @@
     grad_proj, grad_down, grad_up, norm = pl.pallas_call(
         kernel,
         out_shape=(
-            jax.ShapeDtypeStruct((rows, columns), BF16),
+            pltpu.VMEM((rows, columns), BF16),
             jax.ShapeDtypeStruct((3 * ADAPTER_RANK, model // SHARDS), F32),
             jax.ShapeDtypeStruct((ADAPTER_RANK, columns // SHARDS), F32),
             jax.ShapeDtypeStruct((8, HD), F32),
         ),
-        in_specs=[SMEM, HBM, HBM, HBM, HBM, VMEM, VMEM, VMEM, VMEM],
+        in_specs=[SMEM] + [HBM] * 8,
         out_specs=(VMEM, VMEM, VMEM, VMEM),
         scratch_shapes=[
             pltpu.VMEM((rows, model), BF16),
+            pltpu.VMEM((rows, 2 * KVH * HD), BF16),
             pltpu.VMEM((2 * KVH, rows, HD), BF16),
+            pltpu.VMEM((3 * ADAPTER_RANK, model), BF16),
+            pltpu.VMEM((ADAPTER_RANK, columns), BF16),
+            pltpu.VMEM(row_table.shape, F32),
+            pltpu.VMEM(block_table.shape, F32),
             pltpu.VMEM((KVH, rows, width), BF16),
             pltpu.VMEM((KVH, rows, width), BF16),
             pltpu.VMEM((KVH, GROUP_DEV * rows, 2 * HD), BF16),
@@ -565,8 +582,9 @@
             pltpu.VMEM((2, PIECE, HD), F32),
             pltpu.VMEM((PLANE, 8, HD), F32),
             pltpu.VMEM((4, 8, HD), F32),
+            dma((4,)),
             dma,
-            dma((2 * KVH,)),
+            dma,
             dma((2, KVH)),
             dma((KVH, GROUP_DEV - 1)),
             dma((KVH, GROUP_DEV - 1)),
@@ -586,19 +604,24 @@
             dma((4,)),
         ],
         compiler_params=pltpu.CompilerParams(
-            collective_id=0, has_side_effects=True, vmem_limit_bytes=36 * 2**20
+            collective_id=0, has_side_effects=True, vmem_limit_bytes=48 * 2**20
         ),
         name="attention_and_adapter_gradients",
     )(
         shifted_head_flags,
-        normed_layer_input[0],
-        query[0],
-        saved_key_value[0],
-        output_gradient[0],
-        adapter_down_weight,
-        adapter_up_weight,
-        row_table,
-        block_table,
+        *(
+            pltpu.with_memory_space_constraint(array, pltpu.HBM)
+            for array in (
+                normed_layer_input[0],
+                query[0],
+                saved_key_value[0],
+                output_gradient[0],
+                adapter_down_weight,
+                adapter_up_weight,
+                row_table,
+                block_table,
+            )
+        ),
     )
     return (grad_proj[None], grad_down, grad_up, norm[0, 0])
 

time: 92.8 us -> 81.1 us (0.87)
  local copies, waits for them, and re-layouts: 14.7 us -> 4.29 us
  Pallas kernels: 77.1 us -> 76 us
    unnamed x21 -> x5, local copies, waits for them, and re-layouts: 14.2 us -> 3.78 us
    pallas_call x1, Pallas kernels: 77.1 us -> 76 us  [local(): pl.pallas_call(kernel, out_shape=(pltpu.VMEM((rows, columns), BF16), jax....]
where the time goes in v3:
time: 81.1 us; the launch traced here: 80.9 us
  Pallas kernels  76 us (94%)
  local copies, waits for them, and re-layouts  4.29 us (5%)
    pallas_call x1, Pallas kernels, local(): pl.pallas_call(kernel, out_shape=(pltpu.VMEM((rows, columns), BF16), jax....  76 us
    unnamed x5, local copies, waits for them, and re-layouts  3.78 us

profile of v3, /device:TPU:1, one launch (start us, length us, event | category | flops | bytes accessed | tf_op | source)
XLA Modules:
  0.0 80.9 jit_solution(17637702550959852992)
XLA Ops:
  0.6 0.0 copy-start
  0.6 0.6 copy-done
  1.3 76.0 %attention_and_adapter_gradients.1 = (bf16[192,10240]{1,0:T(8,128)(2,1)S(1)}, f32[24,256]{1,0:T(8,128)S(1)}, f32[8,320]{1,0:T(8,128)S(1)}, f32[8,128]{1,0:T(8,128)S(1)}) custom-call(s32[8]{0:T(128)S(1)} %copy-done, bf16[192,8192]{1,0:T(8,128)(2,1)} %bitcast.7, bf16[192,8192]{1,0:T(8,128)(2,1)} %bitcast.8, bf16[192,2048]{1,0:T(8,128)(2,1)} %bitcast.10, ...), custom_call_target="tpu_custom_call" | custom-call | tf_op jit(solution)/shard_map/attention_and_adapter_gradients/pallas_call | solution.py:542
  77.3 0.5 slice.3
  77.8 1.9 %copy.16 = bf16[1,192,10240]{2,1,0:T(8,128)(2,1)} copy(bf16[1,192,10240]{2,1,0:T(8,128)(2,1)S(1)} %bitcast.6) | data formatting | bytes 7864320
  79.7 0.6 copy.17
  80.3 0.6 copy.18
Async XLA Ops:
  0.6 0.7 copy-start

commit v4 on v3

--- a/solution.py
+++ b/solution.py
@@ -167,10 +167,6 @@
     def in_ring(step):
         return lax.rem(y + step, RING)
 
-    def quarter_device(step):
-        code = lax.rem(core * 2 + y_high + step, 4)
-        return device(plane, lax.rem(code, 2) * 2 + y_low, lax.div(code, 2))
-
     mate = device(plane, y, 1 - core)
     barrier = pltpu.get_barrier_semaphore()
 
@@ -183,7 +179,6 @@
     lax.fori_loop(1, PLANE, lambda k, _: (greet(device(in_plane(k), y, core)), 0)[1], 0)
     for step in range(1, RING):
         greet(device(plane, in_ring(step), core))
-        greet(quarter_device(step))
     greet(mate)
 
     copies_in = []
@@ -210,7 +205,7 @@
         window[c, slot, 0:HD] = kv[head]
         window[c, slot, HD : 2 * HD] = kv[head + KVH]
 
-    pl.semaphore_wait(barrier, 2 * (GROUP_DEV - 1) + PLANE - 1 + 2 * (RING - 1) + 1)
+    pl.semaphore_wait(barrier, 2 * (GROUP_DEV - 1) + PLANE - 1 + RING - 1 + 1)
 
     def forward(c, rank, distance):
         part = window.at[c, rank * rows : (rank + 1) * rows]
@@ -429,29 +424,30 @@
 
     sum2[...] = lax.fori_loop(1, PLANE, add_second, total)
 
+    got3[y] = sum2[...]
+
     def third(step):
-        target = in_ring(step)
         return remote(
-            sum2.at[lax.div(target, 2)],
+            got3.at[y],
             got3.at[y],
             send3.at[step],
             recv3.at[y],
-            device(plane, target, core),
+            device(plane, in_ring(step), core),
         )
 
     for step in range(1, RING):
         third(step).start()
-    got3[y] = sum2[y_high]
     for step in range(1, RING):
         source = in_ring(step)
-        remote(sum2.at[0], got3.at[source], send3.at[step], recv3.at[source], mate).wait_recv()
-    mine = got3[0] + got3[1] + got3[2] + got3[3]
-    halves[core] = mine
+        remote(got3.at[source], got3.at[source], send3.at[step], recv3.at[source], mate).wait_recv()
+    whole = got3[0] + got3[1] + got3[2] + got3[3]
+    sum2[...] = whole
+    halves[core] = sum2[y_high]
     fourth = remote(halves.at[core], halves.at[core], send4, recv4, mate)
-    fourth.start()
-    squares = mine * mine
+    squares = whole * whole
     norms[plane] = functools.reduce(
-        lambda a, b: a + b, [squares[8 * r : 8 * (r + 1)] for r in range(PIECE // 8)]
+        lambda a, b: a + b,
+        [squares[h, 8 * r : 8 * (r + 1)] for h in range(2) for r in range(PIECE // 8)],
     )
 
     def fifth(k):
@@ -464,30 +460,20 @@
         return remote(norms.at[source], norms.at[source], send5.at[k], recv5.at[source], mate)
 
     lax.fori_loop(1, PLANE, lambda k, _: (fifth(k).start(), 0)[1], 0)
-    lax.fori_loop(1, PLANE, lambda k, _: (fifth_arrival(k).wait_recv(), 0)[1], 0)
-    code = core * 2 + y_high
-    quarters[code] = jnp.sum(norms[...], axis=0)
-
-    def sixth(step):
-        return remote(
-            quarters.at[code], quarters.at[code], send6.at[step], recv6.at[code], quarter_device(step)
-        )
-
-    for step in range(1, 4):
-        sixth(step).start()
+    fourth.start()
     remote(halves.at[core], halves.at[1 - core], send4, recv4, mate).wait_recv()
     down_out[:, 0:HD] = halves[0, 0:24]
     down_out[:, HD : 2 * HD] = halves[1, 0:24]
     up_out[:, 0:HD] = halves[0, 24:32]
     up_out[:, HD : 2 * HD] = halves[1, 24:32]
     up_out[:, 2 * HD :] = halves[0, 32:40, 0 : up_out.shape[1] - 2 * HD]
-    for step in range(1, 4):
-        source = lax.rem(code + step, 4)
-        remote(
-            quarters.at[source], quarters.at[source], send6.at[step], recv6.at[source], mate
-        ).wait_recv()
-    everything = jnp.sum(jnp.sum(quarters[...], axis=0), keepdims=True)
-    norm_out[...] = jnp.broadcast_to(jnp.sqrt(everything), norm_out.shape)
+    lax.fori_loop(1, PLANE, lambda k, _: (fifth_arrival(k).wait_recv(), 0)[1], 0)
+    quarters[core] = jnp.sum(norms[...], axis=0)
+    sixth = remote(quarters.at[core], quarters.at[core], send6, recv6, mate)
+    sixth.start()
+    remote(quarters.at[1 - core], quarters.at[1 - core], send6, recv6, mate).wait_recv()
+    everything = jnp.sum(quarters[0] + quarters[1], keepdims=True)
+    norm_out[...] = jnp.sqrt(everything)
 
     first.wait_send()
     fourth.wait_send()
@@ -495,7 +481,7 @@
     lax.fori_loop(1, PLANE, lambda k, _: (fifth(k).wait_send(), 0)[1], 0)
     for step in range(1, 4):
         third(step).wait_send()
-        sixth(step).wait_send()
+    sixth.wait_send()
 
     def drain(low, high):
         def wait(i):
@@ -545,7 +531,7 @@
             pltpu.VMEM((rows, columns), BF16),
             jax.ShapeDtypeStruct((3 * ADAPTER_RANK, model // SHARDS), F32),
             jax.ShapeDtypeStruct((ADAPTER_RANK, columns // SHARDS), F32),
-            jax.ShapeDtypeStruct((8, HD), F32),
+            jax.ShapeDtypeStruct((1, 1), F32),
         ),
         in_specs=[SMEM] + [HBM] * 8,
         out_specs=(VMEM, VMEM, VMEM, VMEM),
@@ -578,10 +564,10 @@
             pltpu.VMEM((SHARDS, PIECE, HD), BF16),
             pltpu.VMEM((PLANE, 2, PIECE, HD), BF16),
             pltpu.VMEM((2, PIECE, HD), F32),
-            pltpu.VMEM((RING, PIECE, HD), F32),
+            pltpu.VMEM((RING, 2, PIECE, HD), F32),
             pltpu.VMEM((2, PIECE, HD), F32),
             pltpu.VMEM((PLANE, 8, HD), F32),
-            pltpu.VMEM((4, 8, HD), F32),
+            pltpu.VMEM((2, 8, HD), F32),
             dma((4,)),
             dma,
             dma,
@@ -600,8 +586,8 @@
             dma,
             dma((PLANE,)),
             dma((PLANE,)),
-            dma((4,)),
-            dma((4,)),
+            dma,
+            dma,
         ],
         compiler_params=pltpu.CompilerParams(
             collective_id=0, has_side_effects=True, vmem_limit_bytes=48 * 2**20

time: 81.1 us -> 80.8 us (level)
  between operations: 0.65 us -> 2.42 us
  Pallas kernels: 76 us -> 74.4 us
    pallas_call x1, Pallas kernels: 76 us -> 74.4 us  [local(): pl.pallas_call(kernel, out_shape=(pltpu.VMEM((rows, columns), BF16), jax....]
where the time goes in v4:
time: 80.8 us; the launch traced here: 80.6 us
  Pallas kernels  74.4 us (92%)
  local copies, waits for them, and re-layouts  3.78 us (5%)
  between operations  2.42 us (3%)
    pallas_call x1, Pallas kernels, local(): pl.pallas_call(kernel, out_shape=(pltpu.VMEM((rows, columns), BF16), jax....  74.4 us
    unnamed x5, local copies, waits for them, and re-layouts  3.78 us

profile of v4, /device:TPU:1, one launch (start us, length us, event | category | flops | bytes accessed | tf_op | source)
XLA Modules:
  0.0 80.6 jit_solution(692895078588849221)
XLA Ops:
  0.6 0.0 copy-start
  0.6 0.6 copy-done
  1.3 74.4 %attention_and_adapter_gradients.1 = (bf16[192,10240]{1,0:T(8,128)(2,1)S(1)}, f32[24,256]{1,0:T(8,128)S(1)}, f32[8,320]{1,0:T(8,128)S(1)}, f32[1,1]{1,0:T(1,128)}) custom-call(s32[8]{0:T(128)S(1)} %copy-done, bf16[192,8192]{1,0:T(8,128)(2,1)} %bitcast.7, bf16[192,8192]{1,0:T(8,128)(2,1)} %bitcast.8, bf16[192,2048]{1,0:T(8,128)(2,1)} %bitcast.10, ...), custom_call_target="tpu_custom_call" | custom-call | tf_op jit(solution)/shard_map/attention_and_adapter_gradients/pallas_call | solution.py:528
  75.7 1.9 %copy.17 = bf16[1,192,10240]{2,1,0:T(8,128)(2,1)} copy(bf16[1,192,10240]{2,1,0:T(8,128)(2,1)S(1)} %bitcast.6) | data formatting | bytes 7864320
  77.7 0.6 copy.18
  78.3 0.6 copy.19
Async XLA Ops:
  0.6 0.7 copy-start

commit v5 on v4

--- a/solution.py
+++ b/solution.py
@@ -66,7 +66,7 @@
 
 
 def kernel(
-    flags,
+    flags_hbm,
     x_hbm,
     q_hbm,
     kv_hbm,
@@ -79,6 +79,7 @@
     down_out,
     up_out,
     norm_out,
+    flags,
     xv,
     kv_rows,
     kv,
@@ -98,9 +99,7 @@
     cosines,
     sines,
     low_t,
-    up_heads,
     up,
-    up_class,
     mixed_q,
     packed,
     got1,
@@ -111,6 +110,7 @@
     halves,
     norms,
     quarters,
+    flag_sem,
     small_sem,
     x_sem,
     kv_sem,
@@ -151,6 +151,8 @@
     width_kv = KVH * HD
     rank_a = ADAPTER_RANK
 
+    flags_in = pltpu.make_async_copy(flags_hbm, flags, flag_sem)
+    flags_in.start()
     kv_in = pltpu.make_async_copy(kv_hbm, kv_rows, kv_sem)
     kv_in.start()
 
@@ -193,6 +195,7 @@
         )
     ]
     x_in = pltpu.make_async_copy(x_hbm, xv, x_sem)
+    flags_in.wait()
     kv_in.wait()
     for copy in copies_in + small_in + [x_in]:
         copy.start()
@@ -253,9 +256,6 @@
     row_cos, row_sin = row_table[0], row_table[1]
     cosines[...] = block_cos * row_cos - block_sin * row_sin
     sines[...] = block_sin * row_cos + block_cos * row_sin
-    for h in range(KVH):
-        up_heads[h] = up_w[:, h * width : (h + 1) * width].astype(F32)
-    mixed_q[...] = jnp.zeros_like(mixed_q)
     for copy in copies_in:
         copy.wait()
     x_in.wait()
@@ -314,8 +314,6 @@
             back(c, rank, target).start()
         own[c, :, 0:HD] = key_sum[span - rows :]
         own[c, :, HD : 2 * HD] = value_sum[span - rows :]
-        up_class[c] = adapter_scale * dot(low_of(0), dqs[c], 1, 0)
-        mixed_q[...] += dot(dqs[c], up_heads[head].astype(BF16), 1, 1)
 
     def finish(c, rank):
         total = own[c]
@@ -343,9 +341,15 @@
     pl.when(odd == 1)(lambda: phase(1, 3))
 
     position = positions_of(flags)
+    mixed_sum = None
     for h in range(KVH):
-        grad_proj[:, h * width : (h + 1) * width] = dqs[position[h]]
-        up[:, h * width : (h + 1) * width] = up_class[position[h]]
+        part = slice(h * width, (h + 1) * width)
+        block = dqs[position[h]]
+        grad_proj[:, part] = block
+        up[:, part] = adapter_scale * dot(low_of(0), block, 1, 0)
+        term = dot(block, up_w[:, part], 1, 1)
+        mixed_sum = term if mixed_sum is None else mixed_sum + term
+    mixed_q[...] = mixed_sum
 
     def collect(low, high):
         def last(i):
@@ -473,7 +477,7 @@
     sixth.start()
     remote(quarters.at[1 - core], quarters.at[1 - core], send6, recv6, mate).wait_recv()
     everything = jnp.sum(quarters[0] + quarters[1], keepdims=True)
-    norm_out[...] = jnp.sqrt(everything)
+    norm_out[...] = jnp.broadcast_to(jnp.sqrt(everything), norm_out.shape)
 
     first.wait_send()
     fourth.wait_send()
@@ -531,11 +535,12 @@
             pltpu.VMEM((rows, columns), BF16),
             jax.ShapeDtypeStruct((3 * ADAPTER_RANK, model // SHARDS), F32),
             jax.ShapeDtypeStruct((ADAPTER_RANK, columns // SHARDS), F32),
-            jax.ShapeDtypeStruct((1, 1), F32),
+            jax.ShapeDtypeStruct((8, HD), F32),
         ),
-        in_specs=[SMEM] + [HBM] * 8,
+        in_specs=[HBM] * 9,
         out_specs=(VMEM, VMEM, VMEM, VMEM),
         scratch_shapes=[
+            pltpu.SMEM((KVH,), jnp.int32),
             pltpu.VMEM((rows, model), BF16),
             pltpu.VMEM((rows, 2 * KVH * HD), BF16),
             pltpu.VMEM((2 * KVH, rows, HD), BF16),
@@ -555,9 +560,7 @@
             pltpu.VMEM((rows, HD), F32),
             pltpu.VMEM((rows, HD), F32),
             pltpu.VMEM((3 * ADAPTER_RANK, rows), F32),
-            pltpu.VMEM((KVH, ADAPTER_RANK, width), F32),
             pltpu.VMEM((ADAPTER_RANK, columns), F32),
-            pltpu.VMEM((KVH, ADAPTER_RANK, width), F32),
             pltpu.VMEM((rows, ADAPTER_RANK), F32),
             pltpu.VMEM((2, SHARDS, PIECE, HD), BF16),
             pltpu.VMEM((SHARDS, PIECE, HD), BF16),
@@ -568,6 +571,7 @@
             pltpu.VMEM((2, PIECE, HD), F32),
             pltpu.VMEM((PLANE, 8, HD), F32),
             pltpu.VMEM((2, 8, HD), F32),
+            dma,
             dma((4,)),
             dma,
             dma,
@@ -594,10 +598,10 @@
         ),
         name="attention_and_adapter_gradients",
     )(
-        shifted_head_flags,
         *(
             pltpu.with_memory_space_constraint(array, pltpu.HBM)
             for array in (
+                shifted_head_flags,
                 normed_layer_input[0],
                 query[0],
                 saved_key_value[0],

time: 80.8 us -> 77.7 us (0.962)
  between operations: 2.42 us -> 0.64 us
  Pallas kernels: 74.4 us -> 73.3 us
    pallas_call x1, Pallas kernels: 74.4 us -> 73.3 us  [local(): pl.pallas_call(kernel, out_shape=(pltpu.VMEM((rows, columns), BF16), jax....]
    unnamed x5 -> x3, local copies, waits for them, and re-layouts: 3.78 us -> 3.13 us
where the time goes in v5:
time: 77.7 us; the launch traced here: 77.6 us
  Pallas kernels  73.3 us (94%)
  local copies, waits for them, and re-layouts  3.64 us (5%)
    pallas_call x1, Pallas kernels, local(): pl.pallas_call(kernel, out_shape=(pltpu.VMEM((rows, columns), BF16), jax....  73.3 us
    unnamed x3, local copies, waits for them, and re-layouts  3.13 us

profile of v5, /device:TPU:1, one launch (start us, length us, event | category | flops | bytes accessed | tf_op | source)
XLA Modules:
  0.0 77.6 jit_solution(10496413720195645921)
XLA Ops:
  0.6 73.3 %attention_and_adapter_gradients.1 = (bf16[192,10240]{1,0:T(8,128)(2,1)S(1)}, f32[24,256]{1,0:T(8,128)S(1)}, f32[8,320]{1,0:T(8,128)S(1)}, f32[8,128]{1,0:T(8,128)S(1)}) custom-call(s32[8]{0:T(128)} %flags_hbm.1, bf16[192,8192]{1,0:T(8,128)(2,1)} %bitcast.7, bf16[192,8192]{1,0:T(8,128)(2,1)} %bitcast.8, bf16[192,2048]{1,0:T(8,128)(2,1)} %bitcast.10, ...), custom_call_target="tpu_custom_call" | custom-call | tf_op jit(solution)/shard_map/attention_and_adapter_gradients/pallas_call | solution.py:532
  73.9 0.5 slice.3
  74.4 1.9 %copy.16 = bf16[1,192,10240]{2,1,0:T(8,128)(2,1)} copy(bf16[1,192,10240]{2,1,0:T(8,128)(2,1)S(1)} %bitcast.6) | data formatting | bytes 7864320
  76.4 0.6 copy.17
  77.0 0.6 copy.18

commit v6 on v5

--- a/solution.py
+++ b/solution.py
@@ -258,8 +258,6 @@
     sines[...] = block_sin * row_cos + block_cos * row_sin
     for copy in copies_in:
         copy.wait()
-    x_in.wait()
-    low_t[...] = jnp.transpose(dot(xv[...], down_w[...], 1, 1))
 
     def low_of(segment):
         return low_t[segment * rank_a : (segment + 1) * rank_a].astype(BF16)
@@ -341,6 +339,8 @@
     pl.when(odd == 1)(lambda: phase(1, 3))
 
     position = positions_of(flags)
+    x_in.wait()
+    low_t[...] = jnp.transpose(dot(xv[...], down_w[...], 1, 1))
     mixed_sum = None
     for h in range(KVH):
         part = slice(h * width, (h + 1) * width)
@@ -373,18 +373,6 @@
     down_width = xv.shape[1] // SHARDS
     up_width = up.shape[1] // SHARDS
     zeros = jnp.zeros((8, HD), F32)
-    for shard in range(SHARDS):
-        down = adapter_scale * dot(mixed, xv[:, shard * down_width : (shard + 1) * down_width], 1, 0)
-        mine = up[:, shard * up_width : (shard + 1) * up_width]
-        rest = jnp.concatenate(
-            [mine[:, 2 * HD :], jnp.zeros((8, 3 * HD - up_width), F32)], axis=1
-        )
-        at = packed_place(shard)
-        packed[0, at] = jnp.concatenate([down[:, 0:HD], mine[:, 0:HD], rest, zeros], 0).astype(BF16)
-        packed[1, at] = jnp.concatenate(
-            [down[:, HD:], mine[:, HD : 2 * HD], zeros, zeros], 0
-        ).astype(BF16)
-
     def remote(src, dst, send, recv, target):
         return pltpu.make_async_remote_copy(
             src_ref=src,
@@ -395,9 +383,28 @@
             device_id_type=MESH,
         )
 
-    first = remote(packed.at[1 - core], got1, send1, recv1, mate)
-    first.start()
-    first.wait_recv()
+    def first(chunk):
+        part = slice(chunk * PLANE, (chunk + 1) * PLANE)
+        return remote(
+            packed.at[1 - core, part], got1.at[part], send1.at[chunk], recv1.at[chunk], mate
+        )
+
+    for shard in range(SHARDS):
+        down = adapter_scale * dot(mixed, xv[:, shard * down_width : (shard + 1) * down_width], 1, 0)
+        mine = up[:, shard * up_width : (shard + 1) * up_width]
+        rest = jnp.concatenate(
+            [mine[:, 2 * HD :], jnp.zeros((8, 3 * HD - up_width), F32)], axis=1
+        )
+        at = packed_place(shard)
+        packed[0, at] = jnp.concatenate([down[:, 0:HD], mine[:, 0:HD], rest, zeros], 0).astype(BF16)
+        packed[1, at] = jnp.concatenate(
+            [down[:, HD:], mine[:, HD : 2 * HD], zeros, zeros], 0
+        ).astype(BF16)
+        if shard % PLANE == PLANE - 1:
+            first(shard // PLANE).start()
+
+    for chunk in range(2):
+        first(chunk).wait_recv()
 
     def both(t):
         part = pl.ds(2 * t, 2)
@@ -479,7 +486,8 @@
     everything = jnp.sum(quarters[0] + quarters[1], keepdims=True)
     norm_out[...] = jnp.broadcast_to(jnp.sqrt(everything), norm_out.shape)
 
-    first.wait_send()
+    for chunk in range(2):
+        first(chunk).wait_send()
     fourth.wait_send()
     lax.fori_loop(1, PLANE, lambda k, _: (second(k).wait_send(), 0)[1], 0)
     lax.fori_loop(1, PLANE, lambda k, _: (fifth(k).wait_send(), 0)[1], 0)
@@ -580,8 +588,8 @@
             dma((KVH, GROUP_DEV - 1)),
             dma((KVH, GROUP_DEV - 1)),
             dma((KVH, GROUP_DEV - 1)),
-            dma,
-            dma,
+            dma((2,)),
+            dma((2,)),
             dma((PLANE,)),
             dma((PLANE,)),
             dma((RING,)),

time: 77.7 us -> 77.5 us (level)
  no operation moved by 1% of the time
where the time goes in v6:
time: 77.5 us; the launch traced here: 77.3 us
  Pallas kernels  73.1 us (94%)
  local copies, waits for them, and re-layouts  3.64 us (5%)
    pallas_call x1, Pallas kernels, local(): pl.pallas_call(kernel, out_shape=(pltpu.VMEM((rows, columns), BF16), jax....  73.1 us
    unnamed x3, local copies, waits for them, and re-layouts  3.13 us

profile of v6, /device:TPU:1, one launch (start us, length us, event | category | flops | bytes accessed | tf_op | source)
XLA Modules:
  0.0 77.3 jit_solution(8546013208756672059)
XLA Ops:
  0.6 73.1 %attention_and_adapter_gradients.1 = (bf16[192,10240]{1,0:T(8,128)(2,1)S(1)}, f32[24,256]{1,0:T(8,128)S(1)}, f32[8,320]{1,0:T(8,128)S(1)}, f32[8,128]{1,0:T(8,128)S(1)}) custom-call(s32[8]{0:T(128)} %flags_hbm.1, bf16[192,8192]{1,0:T(8,128)(2,1)} %bitcast.7, bf16[192,8192]{1,0:T(8,128)(2,1)} %bitcast.8, bf16[192,2048]{1,0:T(8,128)(2,1)} %bitcast.10, ...), custom_call_target="tpu_custom_call" | custom-call | tf_op jit(solution)/shard_map/attention_and_adapter_gradients/pallas_call | solution.py:540
  73.7 0.5 slice.3
  74.2 1.9 %copy.16 = bf16[1,192,10240]{2,1,0:T(8,128)(2,1)} copy(bf16[1,192,10240]{2,1,0:T(8,128)(2,1)S(1)} %bitcast.6) | data formatting | bytes 7864320
  76.1 0.6 copy.17
  76.7 0.6 copy.18
